TPU v7x, 256 devices: a whole 4x4x8 slice. The times are simulated.
256 devices in a mesh: tile: 32 (over y, x, z_lo), seq: 8 (over z_hi, core).
Axes of the slice: x: 4, y: 4, z: 8 (z_hi: 4, z_lo: 2; z = z_hi * 2 + z_lo), core: 2. Of those that a mesh axis runs over, the one named last changes fastest.
Arguments:
- latent_rows: bfloat16 [512, 2, 16, 5120], P(('tile', 'seq')), may hold values from -400 to 400
- col_weight: int32 [32, 16], replicated, may hold values from 1 to 16
- row_weight: int32 [32, 16], replicated, may hold values from 1 to 16
- shift_mod: float32 [5120], replicated, may hold values from -3 to 3
- scale_mod: float32 [5120], replicated, may hold values from -3 to 3
- w_query: bfloat16 [5120, 3072], P(None, 'seq'), may hold values from -0.15625 to 0.15625
- w_key: bfloat16 [5120, 3072], P(None, 'seq'), may hold values from -0.078125 to 0.078125
- w_value: bfloat16 [5120, 3072], P(None, 'seq'), may hold values from -0.078125 to 0.078125
Outputs:
- attention: bfloat16 [16384, 3072], P('tile', 'seq')
All inputs are finite; a program needn't handle non-finite values.
Results may differ from a plain program's by a relative error of at most 0.013.
Values may be sent and summed in bfloat16 or wider, within the bound.
No kernel may reach another device: no remote copies, remote signals or barrier semaphores. Data moves between devices by JAX's collectives and lax.ppermute only.
A program may use at most 128 MiB of HBM per device.

v0:
```python
import jax
import jax.numpy as jnp
from jax import lax
from jax.sharding import PartitionSpec as P

HD = 128
GC = 4
OV = 8
OH = 2


def passed_along(shard, axis, by):
    length = lax.axis_size(axis)
    pairs = [(i, i + by) for i in range(length) if 0 <= i + by < length]
    return lax.ppermute(shard, axis, pairs)


def blend_with(own_vals, own_w, head_vals, head_w, tail_vals, tail_w, along):
    full_len = own_vals.shape[along]
    head_len = head_vals.shape[along]
    tail_len = tail_vals.shape[along]
    pad_head = [(0, 0)] * own_vals.ndim
    pad_head[along] = (0, full_len - head_len)
    pad_tail = [(0, 0)] * own_vals.ndim
    pad_tail[along] = (full_len - tail_len, 0)
    heads_full = jnp.pad(head_vals.astype(jnp.float32), pad_head)
    tails_full = jnp.pad(tail_vals.astype(jnp.float32), pad_tail)
    head_wfull = jnp.pad(head_w, (0, full_len - head_len))
    tail_wfull = jnp.pad(tail_w, (full_len - tail_len, 0))
    shape_w = [1] * own_vals.ndim
    shape_w[along] = full_len
    numer = (
        own_vals.astype(jnp.float32) * own_w.reshape(shape_w)
        + heads_full * head_wfull.reshape(shape_w)
        + tails_full * tail_wfull.reshape(shape_w)
    )
    return numer / (own_w + head_wfull + tail_wfull).reshape(shape_w)


def modulate(blended, shift_mod, scale_mod):
    floats = blended.astype(jnp.float32)
    row_mean = jnp.mean(floats, axis=-1, keepdims=True)
    centred = floats - row_mean
    row_var = jnp.mean(centred * centred, axis=-1, keepdims=True)
    return (centred * lax.rsqrt(row_var + 1e-06) * (1.0 + scale_mod) + shift_mod).astype(
        jnp.bfloat16
    )


def attend(token_rows, w_query, w_key, w_value):
    row_count = token_rows.shape[0]
    head_count = w_query.shape[1] // HD
    queries = (
        jnp.dot(token_rows, w_query, preferred_element_type=jnp.float32)
        .astype(jnp.bfloat16)
        .reshape(row_count, head_count, HD)
    )
    key_rows = (
        jnp.dot(token_rows, w_key, preferred_element_type=jnp.float32)
        .astype(jnp.bfloat16)
        .reshape(row_count, head_count, HD)
    )
    values = (
        jnp.dot(token_rows, w_value, preferred_element_type=jnp.float32)
        .astype(jnp.bfloat16)
        .reshape(row_count, head_count, HD)
    )
    scores = jnp.einsum(
        "qhd,khd->hqk", queries, key_rows, preferred_element_type=jnp.float32
    ) * HD ** (-0.5)
    raised = jnp.exp(scores)
    weights_bf = (raised / jnp.sum(raised, axis=-1, keepdims=True)).astype(jnp.bfloat16)
    output = jnp.einsum("hqk,khd->qhd", weights_bf, values, preferred_element_type=jnp.float32)
    return output.astype(jnp.bfloat16).reshape(row_count, head_count * HD)


def take_row(table, index):
    return lax.dynamic_index_in_dim(table, index, 0, keepdims=False)


def local(latent_rows, col_weight, row_weight, shift_mod, scale_mod, w_query, w_key, w_value):
    tile_count = lax.axis_size("tile")
    tile_id = lax.axis_index("tile")
    tile_width = latent_rows.shape[2]
    col_all = col_weight.astype(jnp.float32)
    row_all = row_weight.astype(jnp.float32)
    own_cols = take_row(col_all, tile_id)
    west_on = (tile_id % GC > 0).astype(jnp.float32)
    east_on = (tile_id % GC < GC - 1).astype(jnp.float32)
    west_cols = take_row(col_all, jnp.maximum(tile_id - 1, 0))[tile_width - OV :] * west_on
    east_cols = take_row(col_all, jnp.minimum(tile_id + 1, tile_count - 1))[:OV] * east_on
    own_rows_w = take_row(row_all, tile_id)
    height = own_rows_w.shape[0]
    north_on = (tile_id >= GC).astype(jnp.float32)
    south_on = (tile_id < tile_count - GC).astype(jnp.float32)
    north_rows_w = take_row(row_all, jnp.maximum(tile_id - GC, 0))[height - OH :]
    south_rows_w = take_row(row_all, jnp.minimum(tile_id + GC, tile_count - 1))[:OH]
    whole_tile = lax.all_gather(latent_rows, "seq", axis=0, tiled=True)
    west_part = passed_along(whole_tile[:, :, tile_width - OV :], "tile", 1)
    east_part = passed_along(whole_tile[:, :, :OV], "tile", -1)
    col_mixed = blend_with(
        whole_tile, own_cols, west_part, west_cols, east_part, east_cols, 2
    ).astype(jnp.bfloat16)
    north_part = passed_along(col_mixed[-OH:], "tile", GC)
    south_part = passed_along(col_mixed[:OH], "tile", -GC)
    blended = blend_with(
        col_mixed,
        own_rows_w,
        north_part,
        north_rows_w * north_on,
        south_part,
        south_rows_w * south_on,
        0,
    ).astype(jnp.bfloat16)
    normed = modulate(blended, shift_mod, scale_mod)
    token_rows = normed.reshape(-1, normed.shape[-1])
    return attend(token_rows, w_query, w_key, w_value)


def solution(mesh):
    in_specs = (
        P(("tile", "seq"), None, None, None),
        P(),
        P(),
        P(),
        P(),
        P(None, "seq"),
        P(None, "seq"),
        P(None, "seq"),
    )
    out_specs = P("tile", "seq")
    return jax.shard_map(local, mesh=mesh, in_specs=in_specs, out_specs=out_specs, check_vma=False)
```

profile of v0, /device:TPU:19, one launch (start us, length us, event | category | flops | bytes accessed | tf_op | source)
XLA Modules:
  0.0 263.8 jit_solution(1942900861815577595)
XLA Ops:
  6.5 0.0 all-gather.2.cloned.1.call-start
  6.5 0.7 all-gather.2.cloned.1.call-update
  7.3 0.0 copy-start.3
  7.3 66.8 %all-gather.2.cloned.1.call-done = bf16[16,2,16,5120]{3,2,1,0:T(8,128)(2,1)} async-done(((bf16[2,2,16,5120]{3,2,1,0:T(8,128)(2,1)}), bf16[16,2,16,5120]{3,2,1,0:T(8,128)(2,1)}) %all-gather.2.cloned.1.call-update) | async-done | bytes 5242896 | tf_op jit(solution)/shard_map/all_gather | solution.py:98
  74.1 4.5 %fusion.15 = (bf16[16,2,8,5120]{3,2,1,0:T(8,128)(2,1)}, bf16[16,2,8,5120]{3,2,1,0:T(8,128)(2,1)S(1)}) fusion(bf16[16,2,16,5120]{3,2,1,0:T(8,128)(2,1)} %all-gather.2.cloned.1.call-done), kind=kLoop, calls=%fused_computation.35 | loop fusion | bytes 10485760 | tf_op jit(solution)/shard_map/slice | solution.py:99
  78.6 2.9 %collective-permute-start = (bf16[16,2,8,5120]{3,2,1,0:T(8,128)(2,1)}, bf16[16,2,8,5120]{3,2,1,0:T(8,128)(2,1)}, u32[]{:S(2)}, u32[]{:S(2)}) collective-permute-start(bf16[16,2,8,5120]{3,2,1,0:T(8,128)(2,1)} %get-tuple-element.13), channel_id=1, source_target_pairs={{0,8},{8,16},{16,24},{24,32},{32,40},{40,48},{48,56},{56,64},{64,7... | collective-permute-start | bytes 7864328 | tf_op jit(solution)/shard_map/ppermute | solution.py:15
  81.5 3.3 %collective-permute-start.1 = (bf16[16,2,8,5120]{3,2,1,0:T(8,128)(2,1)S(1)}, bf16[16,2,8,5120]{3,2,1,0:T(8,128)(2,1)}, u32[]{:S(2)}, u32[]{:S(2)}) collective-permute-start(bf16[16,2,8,5120]{3,2,1,0:T(8,128)(2,1)S(1)} %get-tuple-element.14), channel_id=1, source_target_pairs={{8,0},{16,8},{24,16},{32,24},{40,32},{48,40},{56,48},{64,56},{72,6... | collective-permute-start | bytes 7864328 | tf_op jit(solution)/shard_map/ppermute | solution.py:15
  84.8 0.0 copy-done.3
  84.9 0.2 dynamic-slice_reduce_fusion.1
  85.0 0.2 fusion.10
  85.3 0.1 fusion.17
  85.3 54.6 %collective-permute-done = bf16[16,2,8,5120]{3,2,1,0:T(8,128)(2,1)} collective-permute-done((bf16[16,2,8,5120]{3,2,1,0:T(8,128)(2,1)}, bf16[16,2,8,5120]{3,2,1,0:T(8,128)(2,1)}, u32[]{:S(2)}, u32[]{:S(2)}) %collective-permute-start) | collective-permute-done | bytes 2621472 | tf_op jit(solution)/shard_map/ppermute | solution.py:15
  139.9 56.2 %collective-permute-done.1 = bf16[16,2,8,5120]{3,2,1,0:T(8,128)(2,1)} collective-permute-done((bf16[16,2,8,5120]{3,2,1,0:T(8,128)(2,1)S(1)}, bf16[16,2,8,5120]{3,2,1,0:T(8,128)(2,1)}, u32[]{:S(2)}, u32[]{:S(2)}) %collective-permute-start.1) | collective-permute-done | bytes 2621472 | tf_op jit(solution)/shard_map/ppermute | solution.py:15
  196.1 0.0 copy-start.4
  196.1 0.0 copy-start.2
  196.1 6.2 %divide_convert_fusion.1 = bf16[16,2,16,5120]{3,2,1,0:T(8,128)(2,1)S(1)} fusion(bf16[16,2,16,5120]{3,2,1,0:T(8,128)(2,1)} %all-gather.2.cloned.1.call-done, f32[16]{0:T(128)S(1)} %get-tuple-element.19, f32[16]{0:T(128)S(1)} %get-tuple-element.20, bf16[16,2,8,5120]{3,2,1,0:T(8,128)(2,1)} %collective-permute-done.1, f32[16]{0:T(128)S(1)} %get-tuple-element.18, ...), kind=kLoop, calls=%fused_computation.9 | loop fusion | flops 26214400 | bytes 15728896 | tf_op jit(solution)/shard_map/convert_element_type | solution.py:103
  202.3 0.0 copy-start
  202.3 2.3 copy-done
  204.6 0.1 fusion.14
  204.7 3.4 %collective-permute-start.2 = (bf16[2,2,16,5120]{3,2,1,0:T(8,128)(2,1)S(1)}, bf16[2,2,16,5120]{3,2,1,0:T(8,128)(2,1)S(1)}, u32[]{:S(2)}, u32[]{:S(2)}) collective-permute-start(bf16[2,2,16,5120]{3,2,1,0:T(8,128)(2,1)S(1)} %get-tuple-element.11), channel_id=1, source_target_pairs={{0,32},{8,40},{16,48},{24,56},{32,64},{40,72},{48,80},{56,88},{64,... | collective-permute-start | bytes 1966088 | tf_op jit(solution)/shard_map/ppermute | solution.py:15
  208.2 4.3 %collective-permute-start.3 = (bf16[2,2,16,5120]{3,2,1,0:T(8,128)(2,1)S(1)}, bf16[2,2,16,5120]{3,2,1,0:T(8,128)(2,1)S(1)}, u32[]{:S(2)}, u32[]{:S(2)}) collective-permute-start(bf16[2,2,16,5120]{3,2,1,0:T(8,128)(2,1)S(1)} %get-tuple-element.12), channel_id=1, source_target_pairs={{32,0},{40,8},{48,16},{56,24},{64,32},{72,40},{80,48},{88,56},{96,... | collective-permute-start | bytes 1966088 | tf_op jit(solution)/shard_map/ppermute | solution.py:15
  212.5 0.0 copy-done.4
  212.5 0.2 dynamic-slice_reduce_fusion
  212.7 0.2 fusion.12
  212.9 0.1 fusion.16
  213.0 0.0 copy-done.2
  213.0 11.2 %collective-permute-done.2 = bf16[2,2,16,5120]{3,2,1,0:T(8,128)(2,1)S(1)} collective-permute-done((bf16[2,2,16,5120]{3,2,1,0:T(8,128)(2,1)S(1)}, bf16[2,2,16,5120]{3,2,1,0:T(8,128)(2,1)S(1)}, u32[]{:S(2)}, u32[]{:S(2)}) %collective-permute-start.2) | collective-permute-done | bytes 655392 | tf_op jit(solution)/shard_map/ppermute | solution.py:15
  224.2 13.7 %collective-permute-done.3 = bf16[2,2,16,5120]{3,2,1,0:T(8,128)(2,1)S(1)} collective-permute-done((bf16[2,2,16,5120]{3,2,1,0:T(8,128)(2,1)S(1)}, bf16[2,2,16,5120]{3,2,1,0:T(8,128)(2,1)S(1)}, u32[]{:S(2)}, u32[]{:S(2)}) %collective-permute-start.3) | collective-permute-done | bytes 655392 | tf_op jit(solution)/shard_map/ppermute | solution.py:15
  237.9 5.2 %convert_reduce_fusion = (f32[16,2,16]{2,1,0:T(2,128)S(1)}, bf16[16,2,16,5120]{3,2,1,0:T(8,128)(2,1)S(1)}) fusion(f32[16]{0:T(128)S(1)} %get-tuple-element.16, f32[16]{0:T(128)S(1)} %get-tuple-element.17, bf16[2,2,16,5120]{3,2,1,0:T(8,128)(2,1)S(1)} %collective-permute-done.3, f32[16]{0:T(128)S(1)} %get-tuple-element.15, ...), kind=kLoop, calls=%fused_computation.1 | loop fusion | flops 31456768 | bytes 11798784 | tf_op jit(solution)/shard_map/reduce_sum | solution.py:42
  243.2 0.0 copy-start.1
  243.2 1.5 fusion.2
  244.7 0.0 copy-done.1
  244.8 0.0 copy-start.5
  244.8 3.0 %fusion.5 = bf16[16,2,16,5120]{3,2,1,0:T(8,128)(2,1)S(1)} fusion(bf16[16,2,16,5120]{3,2,1,0:T(8,128)(2,1)S(1)} %get-tuple-element.10, f32[5120]{0:T(1024)S(1)} %copy-done.1, f32[5120]{0:T(1024)S(1)} %broadcast_add_fusion, f32[16,2,16]{2,1,0:T(2,128)S(1)} %add_rsqrt_fusion, f32[16,2,16]{2,1,0:T(2,128)S(1)} %broadcast_multiply_fusion), kind=kLoop, calls=%fused_computation.7 | loop fusion | flops 15728640 | bytes 10530816 | tf_op jit(solution)/shard_map/convert_element_type | solution.py:45
  247.8 0.0 copy-done.5
  247.8 0.0 copy-start.6
  247.8 2.3 convolution_convert_fusion.1
  250.1 0.0 copy-done.6
  250.1 0.0 copy-start.7
  250.1 2.3 convolution_convert_fusion
  252.4 0.0 copy-done.7
  252.4 2.2 convolution_convert_fusion.2
  254.6 0.7 fusion.6
  255.3 0.7 fusion.8
  256.1 0.9 copy.20
  (5 shorter events, 0.0 us)
Async XLA Ops:
  6.5 67.6 %all-gather.2.cloned.1.call-start = ((), (), s32[]{:S(2)}) async-start(), calls=%async_computation | async-start | bytes 5898240 | tf_op jit(solution)/shard_map/all_gather | solution.py:98
  7.3 77.6 %copy-start.3 = (s32[32,16]{0,1:T(8,128)S(1)}, s32[32,16]{0,1:T(8,128)}, u32[]{:S(2)}) copy-start(s32[32,16]{0,1:T(8,128)} %param.9) | copy-start | bytes 6148
  78.6 61.3 %collective-permute-start = (bf16[16,2,8,5120]{3,2,1,0:T(8,128)(2,1)}, bf16[16,2,8,5120]{3,2,1,0:T(8,128)(2,1)}, u32[]{:S(2)}, u32[]{:S(2)}) collective-permute-start(bf16[16,2,8,5120]{3,2,1,0:T(8,128)(2,1)} %get-tuple-element.13), channel_id=1, source_target_pairs={{0,8},{8,16},{16,24},{24,32},{32,40},{40,48},{48,56},{56,64},{64,7... | collective-permute-start | bytes 7864328 | tf_op jit(solution)/shard_map/ppermute | solution.py:15
  81.5 114.6 %collective-permute-start.1 = (bf16[16,2,8,5120]{3,2,1,0:T(8,128)(2,1)S(1)}, bf16[16,2,8,5120]{3,2,1,0:T(8,128)(2,1)}, u32[]{:S(2)}, u32[]{:S(2)}) collective-permute-start(bf16[16,2,8,5120]{3,2,1,0:T(8,128)(2,1)S(1)} %get-tuple-element.14), channel_id=1, source_target_pairs={{8,0},{16,8},{24,16},{32,24},{40,32},{48,40},{56,48},{64,56},{72,6... | collective-permute-start | bytes 7864328 | tf_op jit(solution)/shard_map/ppermute | solution.py:15
  196.1 16.4 %copy-start.4 = (s32[32,16]{0,1:T(8,128)S(1)}, s32[32,16]{0,1:T(8,128)}, u32[]{:S(2)}) copy-start(s32[32,16]{0,1:T(8,128)} %param.10) | copy-start | bytes 6148
  196.1 16.9 %copy-start.2 = (f32[5120]{0:T(1024)S(1)}, f32[5120]{0:T(1024)}, u32[]{:S(2)}) copy-start(f32[5120]{0:T(1024)} %param.12) | copy-start | bytes 61444
  202.3 2.3 copy-start
  204.7 19.5 %collective-permute-start.2 = (bf16[2,2,16,5120]{3,2,1,0:T(8,128)(2,1)S(1)}, bf16[2,2,16,5120]{3,2,1,0:T(8,128)(2,1)S(1)}, u32[]{:S(2)}, u32[]{:S(2)}) collective-permute-start(bf16[2,2,16,5120]{3,2,1,0:T(8,128)(2,1)S(1)} %get-tuple-element.11), channel_id=1, source_target_pairs={{0,32},{8,40},{16,48},{24,56},{32,64},{40,72},{48,80},{56,88},{64,... | collective-permute-start | bytes 1966088 | tf_op jit(solution)/shard_map/ppermute | solution.py:15
  208.2 29.8 %collective-permute-start.3 = (bf16[2,2,16,5120]{3,2,1,0:T(8,128)(2,1)S(1)}, bf16[2,2,16,5120]{3,2,1,0:T(8,128)(2,1)S(1)}, u32[]{:S(2)}, u32[]{:S(2)}) collective-permute-start(bf16[2,2,16,5120]{3,2,1,0:T(8,128)(2,1)S(1)} %get-tuple-element.12), channel_id=1, source_target_pairs={{32,0},{40,8},{48,16},{56,24},{64,32},{72,40},{80,48},{88,56},{96,... | collective-permute-start | bytes 1966088 | tf_op jit(solution)/shard_map/ppermute | solution.py:15
  243.2 1.6 copy-start.1
  244.8 3.0 %copy-start.5 = (bf16[5120,384]{1,0:T(8,128)(2,1)S(1)}, bf16[5120,384]{1,0:T(8,128)(2,1)}, u32[]{:S(2)}) copy-start(bf16[5120,384]{1,0:T(8,128)(2,1)} %param.13) | copy-start | bytes 11796484
  247.8 2.3 copy-start.6
  250.1 2.3 copy-start.7
Sparse Core Ops, SparseCore 0:
  9.2 64.8 all-gather.1
where the time goes:
time: 266 us; the launch traced here: 264 us
  waiting for transfers between devices  203 us (76%)
  other arithmetic  16.6 us (6%)
  starting transfers between devices  13.9 us (5%)
  between operations  13.7 us (5%)
  local copies, waits for them, and re-layouts  8.25 us (3%)
  matrix products  8.2 us (3%)
    ppermute x4, waiting for transfers between devices, passed_along(): return lax.ppermute(shard, axis, pairs)  136 us
    all_gather x1, waiting for transfers between devices, local(): whole_tile = lax.all_gather(latent_rows, 'seq', axis=0, tiled=True)  66.8 us
    ppermute x4, starting transfers between devices, passed_along(): return lax.ppermute(shard, axis, pairs)  13.9 us
    convert_element_type x1, other arithmetic, local(): col_mixed = blend_with(whole_tile, own_cols, west_part, west_cols, east_p...  6.21 us
  transfers between devices with their start and end apart: 5, of which 5 were waited for; matrix products, arithmetic and copies ran while one was open for 0% of the time, Pallas kernels for 0%

commit v1 on v0

v1 whole, which is shorter than its diff:
```python
import jax
import jax.numpy as jnp
from jax import lax
from jax.sharding import Mesh, PartitionSpec as P

HD = 128
GC = 4
OV = 8
OH = 2
AX = ("y", "x", "zl", "zh", "c")


def ring(n, by):
    return [(i, (i + by) % n) for i in range(n)]


SWAP = [(0, 1), (1, 0)]
OUTER_PAIRS = [(1, 2), (2, 1), (5, 6), (6, 5)]


def row_pairs():
    pairs = []
    for t in range(28):
        pairs.append((t * 8 + 7, (t + 4) * 8))
        pairs.append(((t + 4) * 8, t * 8 + 7))
    return pairs


def take_row(table, index):
    return lax.dynamic_index_in_dim(table, index, 0, keepdims=False)


def modulate(blended, shift_mod, scale_mod):
    floats = blended.astype(jnp.float32)
    row_mean = jnp.mean(floats, axis=-1, keepdims=True)
    centred = floats - row_mean
    row_var = jnp.mean(centred * centred, axis=-1, keepdims=True)
    return (centred * lax.rsqrt(row_var + 1e-06) * (1.0 + scale_mod) + shift_mod).astype(
        jnp.bfloat16
    )


def local(latent_rows, col_weight, row_weight, shift_mod, scale_mod, w_query, w_key, w_value):
    y, x, zl, zh, c = (lax.axis_index(a) for a in AX)
    tile = y * 8 + x * 2 + zl
    seq = zh * 2 + c
    gcol = tile % GC
    low = zl == 0
    col_all = col_weight.astype(jnp.float32)
    row_all = row_weight.astype(jnp.float32)
    own_cols = take_row(col_all, tile)
    west = take_row(col_all, jnp.maximum(tile - 1, 0))
    east = take_row(col_all, jnp.minimum(tile + 1, 31))
    left, right = latent_rows[:, :, :OV], latent_rows[:, :, OV:]
    outer = jnp.where(low, left, right)
    inner = jnp.where(low, right, left)
    in_other = lax.ppermute(inner, "zl", SWAP)
    out_other = lax.ppermute(outer, ("x", "zl"), OUTER_PAIRS)
    in_w = jnp.where(low, own_cols[OV:], own_cols[:OV])
    in_wo = jnp.where(low, east[:OV], west[OV:])
    out_w = jnp.where(low, own_cols[:OV], own_cols[OV:])
    has_out = ((gcol == 1) | (gcol == 2)).astype(jnp.float32)
    out_wo = jnp.where(low, west[OV:], east[:OV]) * has_out

    def blend(a, wa, b, wb):
        numer = a.astype(jnp.float32) * wa + b.astype(jnp.float32) * wb
        return (numer / (wa + wb)).astype(jnp.bfloat16)

    outer = blend(outer, out_w[:, None], out_other, out_wo[:, None])
    inner = blend(inner, in_w[:, None], in_other, in_wo[:, None])
    both = jnp.stack([outer, inner], 0)
    other = lax.ppermute(both, AX, row_pairs())
    rw = take_row(row_all, tile)
    own_r = lax.dynamic_slice(rw, (2 * seq,), (2,))
    north = take_row(row_all, jnp.maximum(tile - GC, 0))[14:]
    south = take_row(row_all, jnp.minimum(tile + GC, 31))[:OH]
    on_n = ((seq == 0) & (tile >= GC)).astype(jnp.float32)
    on_s = ((seq == 7) & (tile < 28)).astype(jnp.float32)
    oth_r = jnp.where(seq == 0, north * on_n, south * on_s)
    both = blend(both, own_r[None, :, None, None, None], other, oth_r[None, :, None, None, None])
    normed = modulate(both, shift_mod, scale_mod)
    own = normed.reshape(64, -1)

    def weights_on(rows):
        return [
            jnp.dot(rows, w, preferred_element_type=jnp.float32).astype(jnp.bfloat16)
            for w in (w_query, w_key, w_value)
        ]

    def core_swap(v):
        return lax.ppermute(v, "c", SWAP)

    own_x = core_swap(own)
    from_prev = lax.ppermute(own, "zh", ring(4, 1))
    from_next = lax.ppermute(own, "zh", ring(4, -1))
    far_a = lax.ppermute(from_prev[:32], "zh", ring(4, 1))
    far_b = lax.ppermute(from_next[32:], "zh", ring(4, -1))
    mid = jnp.concatenate([from_prev, from_next], 0)
    mid_x = core_swap(mid)
    last = jnp.concatenate([far_a, far_b], 0)
    last_x = core_swap(last)
    parts = [weights_on(v) for v in (own, own_x, mid, mid_x, last, last_x)]

    def joined(k):
        a, ax, m, mx, l, lx = (p[k] for p in parts)
        m, mx = m.reshape(2, 64, -1), mx.reshape(2, 64, -1)
        mine = jnp.stack([a, m[0], m[1], l], 0)
        theirs = jnp.stack([ax, mx[0], mx[1], lx], 0)
        return jnp.stack([mine, theirs], 0).reshape(512, -1, HD)

    q, k, v = joined(0), joined(1), joined(2)
    scores = jnp.einsum("qhd,khd->hqk", q, k, preferred_element_type=jnp.float32) * HD ** (-0.5)
    raised = jnp.exp(scores)
    wts = (raised / jnp.sum(raised, axis=-1, keepdims=True)).astype(jnp.bfloat16)
    out = jnp.einsum("hqk,khd->qhd", wts, v, preferred_element_type=jnp.float32)
    out = out.astype(jnp.bfloat16).reshape(2, 4, 2, 4, 8, -1)
    order = jnp.stack([zh, (zh + 3) % 4, (zh + 1) % 4, (zh + 2) % 4])
    place = jnp.zeros((4,), jnp.int32).at[order].set(jnp.arange(4, dtype=jnp.int32))
    out = jnp.take(out, place, axis=1)
    out = jnp.where(c == 0, out, out[::-1])
    out = jnp.where(low, out, out[:, :, ::-1])
    return out.transpose(1, 0, 3, 2, 4, 5).reshape(512, -1)


def solution(mesh):
    fine = Mesh(mesh.devices.reshape(4, 4, 2, 4, 2), AX)
    in_specs = (
        P(AX, None, None, None),
        P(),
        P(),
        P(),
        P(),
        P(None, ("zh", "c")),
        P(None, ("zh", "c")),
        P(None, ("zh", "c")),
    )
    out_specs = P(("y", "x", "zl"), ("zh", "c"))
    return jax.shard_map(local, mesh=fine, in_specs=in_specs, out_specs=out_specs, check_vma=False)
```

time: 266 us -> 115 us (0.43)
  waiting for transfers between devices: 203 us -> 51.2 us
  starting transfers between devices: 13.9 us -> 39.2 us
  between operations: 13.7 us -> 0.65 us
  other arithmetic: 16.6 us -> 4.64 us
  matrix products: 8.2 us -> 14.9 us
  local copies, waits for them, and re-layouts: 8.25 us -> 4.66 us
    ppermute x4 -> x10, waiting for transfers between devices: 136 us -> 51.2 us  [the longest x1 23 us: local(): from_prev = lax.ppermute(own, 'zh', ring(4, 1))]
    all_gather x1 -> x0, waiting for transfers between devices: 66.8 us -> none  [local(): whole_tile = lax.all_gather(latent_rows, 'seq', axis=0, tiled=True)]
    ppermute x4 -> x10, starting transfers between devices: 13.9 us -> 39.2 us  [the longest x3 25.8 us: core_swap(): return lax.ppermute(v, 'c', SWAP)]
    dot_general x5 -> x20, matrix products: 8.2 us -> 14.9 us  [the longest x18 13.5 us: weights_on(): jnp.dot(rows, w, preferred_element_type=jnp.float32).astype(jnp.bfloat16)]
    convert_element_type x1 -> x0, other arithmetic: 6.21 us -> none  [local(): col_mixed = blend_with(whole_tile, own_cols, west_part, west_cols, east_p...]
    reduce_sum x1, other arithmetic: 5.24 us -> 0.48 us  [modulate(): row_mean = jnp.mean(floats, axis=-1, keepdims=True)]
    slice x2 -> x8, local copies, waits for them, and re-layouts: 4.62 us -> 0.12 us  [the longest x3 0.04 us: joined(): theirs = jnp.stack([ax, mx[0], mx[1], lx], 0)]
    convert_element_type x1, other arithmetic: 3.01 us -> 0.3 us  [modulate(): (centred * lax.rsqrt(row_var + 1e-06) * (1.0 + scale_mod) + shift_mod).as...]
  transfers between devices with their start and end apart: 5 -> 10, of which waited for: 5 -> 6; matrix products, arithmetic and copies ran while one was open for 0% -> 12% of each run, Pallas kernels for 0% -> 0%
where the time goes in v1:
time: 115 us
  waiting for transfers between devices  51.2 us (45%)
  starting transfers between devices  39.2 us (34%)
  matrix products  14.9 us (13%)
  local copies, waits for them, and re-layouts  4.66 us (4%)
  other arithmetic  4.64 us (4%)
    ppermute x3, starting transfers between devices, core_swap(): return lax.ppermute(v, 'c', SWAP)  25.8 us
    ppermute x1, waiting for transfers between devices, local(): from_prev = lax.ppermute(own, 'zh', ring(4, 1))  23 us
    ppermute x1, waiting for transfers between devices, local(): far_a = lax.ppermute(from_prev[:32], 'zh', ring(4, 1))  14.8 us
    dot_general x18, matrix products, weights_on(): jnp.dot(rows, w, preferred_element_type=jnp.float32).astype(jnp.bfloat16)  13.5 us
    ppermute x1, waiting for transfers between devices, local(): out_other = lax.ppermute(outer, ('x', 'zl'), OUTER_PAIRS)  6.06 us
    ppermute x1, waiting for transfers between devices, local(): in_other = lax.ppermute(inner, 'zl', SWAP)  5.32 us
    ppermute x1, starting transfers between devices, local(): far_b = lax.ppermute(from_next[32:], 'zh', ring(4, -1))  4.39 us
    ppermute x1, starting transfers between devices, local(): from_next = lax.ppermute(own, 'zh', ring(4, -1))  4.37 us
  transfers between devices with their start and end apart: 10, of which 6 were waited for; matrix products, arithmetic and copies ran while one was open for 12% of the time, Pallas kernels for 0%

profile of v1, /device:TPU:19, one launch (start us, length us, event | category | flops | bytes accessed | tf_op | source)
XLA Modules:
  0.0 115.2 jit_solution(334608747370382866)
XLA Ops:
  0.0 1.1 broadcast_select_fusion.1
  1.2 3.5 %collective-permute-start = (bf16[2,2,8,5120]{3,2,1,0:T(8,128)(2,1)S(1)}, bf16[2,2,8,5120]{3,2,1,0:T(8,128)(2,1)S(1)}, u32[]{:S(2)}, u32[]{:S(2)}) collective-permute-start(bf16[2,2,8,5120]{3,2,1,0:T(8,128)(2,1)S(1)} %get-tuple-element.13), channel_id=1, source_target_pairs={{8,16},{16,8},{40,48},{48,40},{9,17},{17,9},{41,49},{49,41},{10,18... | collective-permute-start | bytes 983048 | tf_op jit(solution)/shard_map/ppermute | solution.py:58
  4.8 0.7 convert_element_type.112
  5.6 0.6 scatter_custom_fusion
  6.2 0.2 multiply_reduce_fusion
  6.5 6.1 %collective-permute-done = bf16[2,2,8,5120]{3,2,1,0:T(8,128)(2,1)S(1)} collective-permute-done((bf16[2,2,8,5120]{3,2,1,0:T(8,128)(2,1)S(1)}, bf16[2,2,8,5120]{3,2,1,0:T(8,128)(2,1)S(1)}, u32[]{:S(2)}, u32[]{:S(2)}) %collective-permute-start) | collective-permute-done | bytes 327712 | tf_op jit(solution)/shard_map/ppermute | solution.py:58
  12.5 0.2 fusion.27
  12.7 5.3 %collective-permute-done.1 = bf16[2,2,8,5120]{3,2,1,0:T(8,128)(2,1)S(1)} collective-permute-done((bf16[2,2,8,5120]{3,2,1,0:T(8,128)(2,1)S(1)}, bf16[2,2,8,5120]{3,2,1,0:T(8,128)(2,1)S(1)}, u32[]{:S(2)}, u32[]{:S(2)}) %collective-permute-start.1) | collective-permute-done | bytes 327712 | tf_op jit(solution)/shard_map/ppermute | solution.py:57
  18.1 0.2 fusion.28
  18.3 0.7 collective-permute-start.2
  19.4 0.5 convert_reduce_fusion
  19.9 0.3 fusion.4
  20.3 0.3 fusion.7
  20.6 23.3 %collective-permute-start.7 = (bf16[64,5120]{1,0:T(8,128)(2,1)S(1)}, bf16[64,5120]{1,0:T(8,128)(2,1)S(1)}, u32[]{:S(2)}, u32[]{:S(2)}) collective-permute-start(bf16[64,5120]{1,0:T(8,128)(2,1)S(1)} %bitcast.121), channel_id=1, source_target_pairs={{0,1},{1,0},{2,3},{3,2},{4,5},{5,4},{6,7},{7,6},{8,9},{9,8},{10,11... | collective-permute-start | bytes 1966088 | tf_op jit(solution)/shard_map/ppermute | solution.py:91
  43.9 4.4 %collective-permute-start.4 = (bf16[64,5120]{1,0:T(8,128)(2,1)S(1)}, bf16[64,5120]{1,0:T(8,128)(2,1)S(1)}, u32[]{:S(2)}, u32[]{:S(2)}) collective-permute-start(bf16[64,5120]{1,0:T(8,128)(2,1)S(1)} %bitcast.122), channel_id=1, source_target_pairs={{0,6},{2,0},{4,2},{6,4},{1,7},{3,1},{5,3},{7,5},{8,14},{10,8},{12,... | collective-permute-start | bytes 1966088 | tf_op jit(solution)/shard_map/ppermute | solution.py:95
  48.3 0.7 fusion.18
  49.0 0.7 fusion.14
  49.7 1.4 %copy-done.1 = bf16[5120,384]{1,0:T(8,128)(2,1)S(1)} copy-done((bf16[5120,384]{1,0:T(8,128)(2,1)S(1)}, bf16[5120,384]{1,0:T(8,128)(2,1)}, u32[]{:S(2)}) %copy-start.1) | copy-done | bytes 3932184
  51.1 0.7 fusion.10
  51.8 23.0 %collective-permute-done.3 = bf16[64,5120]{1,0:T(8,128)(2,1)S(1)} collective-permute-done((bf16[64,5120]{1,0:T(8,128)(2,1)S(1)}, bf16[64,5120]{1,0:T(8,128)(2,1)S(1)}, u32[]{:S(2)}, u32[]{:S(2)}) %collective-permute-start.3) | collective-permute-done | bytes 655392 | tf_op jit(solution)/shard_map/ppermute | solution.py:94
  74.8 1.1 collective-permute-done.4
  75.9 0.9 convolution_convert_fusion.1
  76.8 0.9 convolution_convert_fusion.3
  77.6 1.3 %collective-permute-start.8 = (bf16[128,5120]{1,0:T(8,128)(2,1)S(1)}, bf16[128,5120]{1,0:T(8,128)(2,1)S(1)}, u32[]{:S(2)}, u32[]{:S(2)}) collective-permute-start(bf16[128,5120]{1,0:T(8,128)(2,1)S(1)} %constant_dynamic-update-slice_fusion), channel_id=1, source_target_pairs={{0,1},{1,0},{2,3},{3,2},{4,5},{5,4},{6,7},{7,6},{8,9},{9,8},{10,11... | collective-permute-start | bytes 3932168 | tf_op jit(solution)/shard_map/ppermute | solution.py:91
  79.0 4.4 %collective-permute-start.6 = (bf16[32,5120]{1,0:T(8,128)(2,1)S(1)}, bf16[32,5120]{1,0:T(8,128)(2,1)S(1)}, u32[]{:S(2)}, u32[]{:S(2)}) collective-permute-start(bf16[32,5120]{1,0:T(8,128)(2,1)S(1)} %slice.151), channel_id=1, source_target_pairs={{0,6},{2,0},{4,2},{6,4},{1,7},{3,1},{5,3},{7,5},{8,14},{10,8},{12,... | collective-permute-start | bytes 983048 | tf_op jit(solution)/shard_map/ppermute | solution.py:97
  83.4 0.3 collective-permute-start.5
  83.7 0.9 convolution_convert_fusion.5
  84.6 0.7 fusion.20
  85.3 0.7 fusion.16
  86.0 0.7 fusion.12
  86.7 14.8 %collective-permute-done.5 = bf16[32,5120]{1,0:T(8,128)(2,1)S(1)} collective-permute-done((bf16[32,5120]{1,0:T(8,128)(2,1)S(1)}, bf16[32,5120]{1,0:T(8,128)(2,1)S(1)}, u32[]{:S(2)}, u32[]{:S(2)}) %collective-permute-start.5) | collective-permute-done | bytes 327712 | tf_op jit(solution)/shard_map/ppermute | solution.py:96
  101.6 0.7 fusion.19
  102.4 0.7 fusion.15
  103.1 1.2 %collective-permute-start.9 = (bf16[64,5120]{1,0:T(8,128)(2,1)S(1)}, bf16[64,5120]{1,0:T(8,128)(2,1)S(1)}, u32[]{:S(2)}, u32[]{:S(2)}) collective-permute-start(bf16[64,5120]{1,0:T(8,128)(2,1)S(1)} %constant_dynamic-update-slice_fusion.2), channel_id=1, source_target_pairs={{0,1},{1,0},{2,3},{3,2},{4,5},{5,4},{6,7},{7,6},{8,9},{9,8},{10,11... | collective-permute-start | bytes 1966088 | tf_op jit(solution)/shard_map/ppermute | solution.py:91
  104.3 0.7 fusion.11
  105.1 0.9 collective-permute-done.9
  106.0 0.7 fusion.21
  106.7 0.7 fusion.17
  107.4 0.7 fusion.13
  108.2 0.9 convolution_convert_fusion
  109.0 0.9 convolution_convert_fusion.4
  109.9 0.9 convolution_convert_fusion.2
  111.4 0.7 fusion
  112.1 0.7 fusion.9
  112.8 0.3 copy.23
  113.1 0.3 reshape.343
  113.5 0.6 gather_fusion
  114.4 0.8 copy.24
  (58 shorter events, 1.7 us)
Async XLA Ops:
  0.0 19.1 %copy-start.5 = (s32[32,16]{0,1:T(8,128)S(1)}, s32[32,16]{0,1:T(8,128)}, u32[]{:S(2)}) copy-start(s32[32,16]{0,1:T(8,128)} %param.10) | copy-start | bytes 6148
  0.0 19.4 %copy-start.3 = (f32[5120]{0:T(1024)S(1)}, f32[5120]{0:T(1024)}, u32[]{:S(2)}) copy-start(f32[5120]{0:T(1024)} %param.12) | copy-start | bytes 61444
  1.1 19.1 %copy-start.4 = (f32[5120]{0:T(1024)S(1)}, f32[5120]{0:T(1024)}, u32[]{:S(2)}) copy-start(f32[5120]{0:T(1024)} %param.11) | copy-start | bytes 61444
  1.2 11.4 %collective-permute-start = (bf16[2,2,8,5120]{3,2,1,0:T(8,128)(2,1)S(1)}, bf16[2,2,8,5120]{3,2,1,0:T(8,128)(2,1)S(1)}, u32[]{:S(2)}, u32[]{:S(2)}) collective-permute-start(bf16[2,2,8,5120]{3,2,1,0:T(8,128)(2,1)S(1)} %get-tuple-element.13), channel_id=1, source_target_pairs={{8,16},{16,8},{40,48},{48,40},{9,17},{17,9},{41,49},{49,41},{10,18... | collective-permute-start | bytes 983048 | tf_op jit(solution)/shard_map/ppermute | solution.py:58
  4.7 13.4 %collective-permute-start.1 = (bf16[2,2,8,5120]{3,2,1,0:T(8,128)(2,1)S(1)}, bf16[2,2,8,5120]{3,2,1,0:T(8,128)(2,1)S(1)}, u32[]{:S(2)}, u32[]{:S(2)}) collective-permute-start(bf16[2,2,8,5120]{3,2,1,0:T(8,128)(2,1)S(1)} %get-tuple-element.14), channel_id=1, source_target_pairs={{0,8},{8,0},{1,9},{9,1},{2,10},{10,2},{3,11},{11,3},{4,12},{12,4},... | collective-permute-start | bytes 983048 | tf_op jit(solution)/shard_map/ppermute | solution.py:57
  18.3 1.1 collective-permute-start.2
  19.1 29.1 %copy-start = (bf16[5120,384]{1,0:T(8,128)(2,1)S(1)}, bf16[5120,384]{1,0:T(8,128)(2,1)}, u32[]{:S(2)}) copy-start(bf16[5120,384]{1,0:T(8,128)(2,1)} %param.14) | copy-start | bytes 11796484
  20.2 28.7 %copy-start.2 = (bf16[5120,384]{1,0:T(8,128)(2,1)S(1)}, bf16[5120,384]{1,0:T(8,128)(2,1)}, u32[]{:S(2)}) copy-start(bf16[5120,384]{1,0:T(8,128)(2,1)} %param.13) | copy-start | bytes 11796484
  20.6 64.0 %collective-permute-start.7 = (bf16[64,5120]{1,0:T(8,128)(2,1)S(1)}, bf16[64,5120]{1,0:T(8,128)(2,1)S(1)}, u32[]{:S(2)}, u32[]{:S(2)}) collective-permute-start(bf16[64,5120]{1,0:T(8,128)(2,1)S(1)} %bitcast.121), channel_id=1, source_target_pairs={{0,1},{1,0},{2,3},{3,2},{4,5},{5,4},{6,7},{7,6},{8,9},{9,8},{10,11... | collective-permute-start | bytes 1966088 | tf_op jit(solution)/shard_map/ppermute | solution.py:91
  43.9 32.0 %collective-permute-start.4 = (bf16[64,5120]{1,0:T(8,128)(2,1)S(1)}, bf16[64,5120]{1,0:T(8,128)(2,1)S(1)}, u32[]{:S(2)}, u32[]{:S(2)}) collective-permute-start(bf16[64,5120]{1,0:T(8,128)(2,1)S(1)} %bitcast.122), channel_id=1, source_target_pairs={{0,6},{2,0},{4,2},{6,4},{1,7},{3,1},{5,3},{7,5},{8,14},{10,8},{12,... | collective-permute-start | bytes 1966088 | tf_op jit(solution)/shard_map/ppermute | solution.py:95
  48.2 26.5 %collective-permute-start.3 = (bf16[64,5120]{1,0:T(8,128)(2,1)S(1)}, bf16[64,5120]{1,0:T(8,128)(2,1)S(1)}, u32[]{:S(2)}, u32[]{:S(2)}) collective-permute-start(bf16[64,5120]{1,0:T(8,128)(2,1)S(1)} %bitcast.123), channel_id=1, source_target_pairs={{0,2},{2,4},{4,6},{6,0},{1,3},{3,5},{5,7},{7,1},{8,10},{10,12},{12... | collective-permute-start | bytes 1966088 | tf_op jit(solution)/shard_map/ppermute | solution.py:94
  49.0 2.1 %copy-start.1 = (bf16[5120,384]{1,0:T(8,128)(2,1)S(1)}, bf16[5120,384]{1,0:T(8,128)(2,1)}, u32[]{:S(2)}) copy-start(bf16[5120,384]{1,0:T(8,128)(2,1)} %param.15) | copy-start | bytes 11796484
  77.6 30.5 %collective-permute-start.8 = (bf16[128,5120]{1,0:T(8,128)(2,1)S(1)}, bf16[128,5120]{1,0:T(8,128)(2,1)S(1)}, u32[]{:S(2)}, u32[]{:S(2)}) collective-permute-start(bf16[128,5120]{1,0:T(8,128)(2,1)S(1)} %constant_dynamic-update-slice_fusion), channel_id=1, source_target_pairs={{0,1},{1,0},{2,3},{3,2},{4,5},{5,4},{6,7},{7,6},{8,9},{9,8},{10,11... | collective-permute-start | bytes 3932168 | tf_op jit(solution)/shard_map/ppermute | solution.py:91
  79.0 22.6 %collective-permute-start.6 = (bf16[32,5120]{1,0:T(8,128)(2,1)S(1)}, bf16[32,5120]{1,0:T(8,128)(2,1)S(1)}, u32[]{:S(2)}, u32[]{:S(2)}) collective-permute-start(bf16[32,5120]{1,0:T(8,128)(2,1)S(1)} %slice.151), channel_id=1, source_target_pairs={{0,6},{2,0},{4,2},{6,4},{1,7},{3,1},{5,3},{7,5},{8,14},{10,8},{12,... | collective-permute-start | bytes 983048 | tf_op jit(solution)/shard_map/ppermute | solution.py:97
  83.4 18.1 %collective-permute-start.5 = (bf16[32,5120]{1,0:T(8,128)(2,1)S(1)}, bf16[32,5120]{1,0:T(8,128)(2,1)S(1)}, u32[]{:S(2)}, u32[]{:S(2)}) collective-permute-start(bf16[32,5120]{1,0:T(8,128)(2,1)S(1)} %slice.150), channel_id=1, source_target_pairs={{0,2},{2,4},{4,6},{6,0},{1,3},{3,5},{5,7},{7,1},{8,10},{10,12},{12... | collective-permute-start | bytes 983048 | tf_op jit(solution)/shard_map/ppermute | solution.py:96
  103.1 2.9 %collective-permute-start.9 = (bf16[64,5120]{1,0:T(8,128)(2,1)S(1)}, bf16[64,5120]{1,0:T(8,128)(2,1)S(1)}, u32[]{:S(2)}, u32[]{:S(2)}) collective-permute-start(bf16[64,5120]{1,0:T(8,128)(2,1)S(1)} %constant_dynamic-update-slice_fusion.2), channel_id=1, source_target_pairs={{0,1},{1,0},{2,3},{3,2},{4,5},{5,4},{6,7},{7,6},{8,9},{9,8},{10,11... | collective-permute-start | bytes 1966088 | tf_op jit(solution)/shard_map/ppermute | solution.py:91

commit v2 on v1

v2 whole, which is shorter than its diff:
```python
import jax
import jax.numpy as jnp
from jax import lax
from jax.experimental import pallas as pl
from jax.experimental.pallas import tpu as pltpu
from jax.sharding import Mesh, PartitionSpec as P

HD = 128
GC = 4
OV = 8
OH = 2
AX = ("y", "x", "zl", "zh", "c")
SLOTS = 4


OUTER_PAIRS = [(1, 2), (2, 1), (5, 6), (6, 5)]
SWAP = [(0, 1), (1, 0)]


def ring(by):
    return [(g, (g + by) % 4) for g in range(4)]


def row_pairs(neighbour):
    pairs = []
    for t in range(32 - GC):
        n = neighbour(t)
        if n is not None:
            pairs.append((n * 8 + 7, (t + GC) * 8))
            pairs.append(((n + GC) * 8, t * 8 + 7))
    return pairs


def itself(t):
    return t


def inner_of(t):
    return t ^ 1


def outer_of(t):
    return {0: None, 1: t + 1, 2: t - 1, 3: None}[t % GC]


def take_row(table, index):
    return lax.dynamic_index_in_dim(table, index, 0, keepdims=False)


def modulate(blended, shift_mod, scale_mod):
    floats = blended.astype(jnp.float32)
    row_mean = jnp.mean(floats, axis=-1, keepdims=True)
    centred = floats - row_mean
    row_var = jnp.mean(centred * centred, axis=-1, keepdims=True)
    return (centred * lax.rsqrt(row_var + 1e-06) * (1.0 + scale_mod) + shift_mod).astype(
        jnp.bfloat16
    )


def blend(a, wa, b, wb):
    numer = a.astype(jnp.float32) * wa + b.astype(jnp.float32) * wb
    return (numer / (wa + wb)).astype(jnp.bfloat16)


def local(latent_rows, col_weight, row_weight, shift_mod, scale_mod, w_query, w_key, w_value):
    y, x, zl, zh, c = (lax.axis_index(a) for a in AX)
    tile = y * 8 + x * 2 + zl
    gcol = tile % GC
    low = zl == 0
    top_here = (zh == 0) & (c == 0) & (tile >= GC)
    bottom_here = (zh == 3) & (c == 1) & (tile < 32 - GC)
    col_all = col_weight.astype(jnp.float32)
    row_all = row_weight.astype(jnp.float32)
    partner = jnp.where(zh == 0, jnp.maximum(tile - GC, 0), jnp.minimum(tile + GC, 31))
    left, right = latent_rows[:, :, :OV], latent_rows[:, :, OV:]
    outer = jnp.where(low, left, right)
    inner = jnp.where(low, right, left)

    def col_mix(t, v, out_other, in_other):
        own_cols = take_row(col_all, t)
        west = take_row(col_all, jnp.maximum(t - 1, 0))[OV:] * (gcol > 0)
        east = take_row(col_all, jnp.minimum(t + 1, 31))[:OV] * (gcol < GC - 1)
        other = jnp.concatenate(
            [jnp.where(low, out_other, in_other), jnp.where(low, in_other, out_other)], 2
        )
        return blend(v, own_cols[:, None], other, jnp.concatenate([west, east])[:, None])

    far_rows = lax.ppermute(latent_rows, AX, row_pairs(itself))
    far_outer = lax.ppermute(outer, AX, row_pairs(outer_of))
    far_inner = lax.ppermute(inner, AX, row_pairs(inner_of))
    out_other = lax.ppermute(outer, ("x", "zl"), OUTER_PAIRS)
    in_other = lax.ppermute(inner, "zl", SWAP)
    own = col_mix(tile, latent_rows, out_other, in_other)
    other = col_mix(partner, far_rows, far_outer, far_inner)
    own_r = lax.dynamic_slice(take_row(row_all, tile), (4 * zh + 2 * c,), (OH,))
    other_r = take_row(row_all, partner)
    other_r = jnp.where(zh == 0, other_r[14:], other_r[:OH]) * (top_here | bottom_here)
    own = blend(own, own_r[:, None, None, None], other, other_r[:, None, None, None])
    own = modulate(own, shift_mod, scale_mod).reshape(64, -1)

    def core_swap(v):
        return lax.ppermute(v, "c", SWAP)

    def weights_on(rows):
        return [
            jnp.dot(rows, w, preferred_element_type=jnp.float32).astype(jnp.bfloat16)
            for w in (w_query, w_key, w_value)
        ]

    def both_cores(v):
        return jnp.concatenate([v, core_swap(v)], 0)

    prev = lax.ppermute(own, "zh", ring(1))
    nxt = lax.ppermute(own, "zh", ring(-1))
    own_q = weights_on(both_cores(own))
    prev, nxt, *own_q = lax.optimization_barrier((prev, nxt, *own_q))
    side = jnp.concatenate([prev, nxt], 0)
    far = [lax.ppermute(side[:32], "zh", ring(1)), lax.ppermute(side[96:], "zh", ring(-1))]
    side_q, side_x = weights_on(side), weights_on(core_swap(side))
    *far, side_q, side_x = lax.optimization_barrier((*far, side_q, side_x))
    far = jnp.concatenate(far, 0)
    far_q = weights_on(both_cores(far))
    at = [
        (((zh - d) % 4) * 2 + core) * 64 for core in (c, 1 - c) for d in (0, 1, 3, 2)
    ]
    return attention(jnp.stack(at).astype(jnp.int32), own_q, side_q, side_x, far_q)


def attention_kernel(at, *refs):
    parts, (out, *wholes) = refs[:12], refs[12:]

    def put(whole, n, rows):
        whole[pl.ds(pl.multiple_of(at[n], 64), 64), :] = rows

    for n, whole in enumerate(wholes):
        own, side, side_x, far = parts[n::3]
        for core, pair in enumerate((side, side_x)):
            rows = slice(core * 64, core * 64 + 64)
            put(whole, core * 4, own[rows, :])
            put(whole, core * 4 + 1, pair[:64, :])
            put(whole, core * 4 + 2, pair[64:, :])
            put(whole, core * 4 + 3, far[rows, :])
    q_all, k_all, v_all = wholes
    for h in range(out.shape[1] // HD):
        cols = slice(h * HD, h * HD + HD)
        scores = lax.dot_general(
            q_all[:, cols],
            k_all[:, cols],
            (((1,), (1,)), ((), ())),
            preferred_element_type=jnp.float32,
        ) * HD ** (-0.5)
        raised = jnp.exp(scores)
        wts = (raised / jnp.sum(raised, axis=-1, keepdims=True)).astype(jnp.bfloat16)
        out[:, cols] = jnp.dot(
            wts, v_all[:, cols], preferred_element_type=jnp.float32
        ).astype(jnp.bfloat16)


def attention(at, *groups):
    width = groups[0][0].shape[1]
    here = pl.BlockSpec(memory_space=pltpu.VMEM)
    return pl.pallas_call(
        attention_kernel,
        out_shape=jax.ShapeDtypeStruct((512, width), jnp.bfloat16),
        in_specs=[pl.BlockSpec(memory_space=pltpu.SMEM)] + [here] * 12,
        out_specs=here,
        scratch_shapes=[pltpu.VMEM((512, width), jnp.bfloat16)] * 3,
        compiler_params=pltpu.CompilerParams(vmem_limit_bytes=12 * 1024 * 1024),
    )(at, *(v for g in groups for v in g))


def solution(mesh):
    fine = Mesh(mesh.devices.reshape(4, 4, 2, 4, 2), AX)
    in_specs = (
        P(AX, None, None, None),
        P(),
        P(),
        P(),
        P(),
        P(None, ("zh", "c")),
        P(None, ("zh", "c")),
        P(None, ("zh", "c")),
    )
    out_specs = P(("y", "x", "zl"), ("zh", "c"))
    return jax.shard_map(local, mesh=fine, in_specs=in_specs, out_specs=out_specs, check_vma=False)
```

time: 115 us -> 105 us (0.913)
  the two profiles are of different devices: /device:TPU:19 before, /device:TPU:9 now
where the time goes in v2:
time: 105 us
  waiting for transfers between devices  40.1 us (38%)
  starting transfers between devices  38.1 us (36%)
  matrix products  12.9 us (12%)
  local copies, waits for them, and re-layouts  7.11 us (7%)
  other arithmetic  3.33 us (3%)
  Pallas kernels  2.73 us (3%)
    ppermute x3, starting transfers between devices, core_swap(): return lax.ppermute(v, 'c', SWAP)  22.7 us
    ppermute x1, waiting for transfers between devices, local(): prev = lax.ppermute(own, 'zh', ring(1))  21.5 us
    dot_general x12, matrix products, weights_on(): jnp.dot(rows, w, preferred_element_type=jnp.float32).astype(jnp.bfloat16)  12.9 us
    ppermute x1, waiting for transfers between devices, local(): in_other = lax.ppermute(inner, 'zl', SWAP)  9.8 us
    unnamed x29, local copies, waits for them, and re-layouts  4.76 us
    ppermute x1, starting transfers between devices, local(): lax.ppermute(side[:32], 'zh', ring(1))  4.43 us
    ppermute x1, starting transfers between devices, local(): nxt = lax.ppermute(own, 'zh', ring(-1))  4.39 us
    ppermute x1, waiting for transfers between devices, local(): lax.ppermute(side[:32], 'zh', ring(1))  3.99 us
  transfers between devices with their start and end apart: 12, of which 5 were waited for; matrix products, arithmetic and copies ran while one was open for 14% of the time, Pallas kernels for 0%

profile of v2, /device:TPU:9, one launch (start us, length us, event | category | flops | bytes accessed | tf_op | source)
XLA Modules:
  0.0 104.6 jit_solution(11226370634063970638)
XLA Ops:
  0.0 0.8 collective-permute-start.2
  0.9 1.1 %broadcast_select_fusion.5 = (bf16[2,2,8,5120]{3,2,1,0:T(8,128)(2,1)S(1)}, bf16[2,2,8,5120]{3,2,1,0:T(8,128)(2,1)S(1)}) fusion(pred[]{:T(512)S(6)} %eq.27, bf16[2,2,16,5120]{3,2,1,0:T(8,128)(2,1)} %param.8), kind=kLoop, calls=%fused_computation.30 | loop fusion | flops 327680 | bytes 1310721 | tf_op jit(solution)/shard_map/jit(_where)/select_n | solution.py:76
  2.0 0.7 collective-permute-start.3
  2.7 0.7 collective-permute-start
  3.4 0.7 collective-permute-start.4
  4.1 3.7 %collective-permute-start.1 = (bf16[2,2,8,5120]{3,2,1,0:T(8,128)(2,1)S(1)}, bf16[2,2,8,5120]{3,2,1,0:T(8,128)(2,1)S(1)}, u32[]{:S(2)}, u32[]{:S(2)}) collective-permute-start(bf16[2,2,8,5120]{3,2,1,0:T(8,128)(2,1)S(1)} %get-tuple-element.50), channel_id=1, source_target_pairs={{0,8},{8,0},{1,9},{9,1},{2,10},{10,2},{3,11},{11,3},{4,12},{12,4},... | collective-permute-start | bytes 983048 | tf_op jit(solution)/shard_map/ppermute | solution.py:92
  7.8 0.2 dynamic-slice_reduce_fusion.1
  8.0 0.2 fusion.9
  8.2 0.1 fusion.16
  8.3 0.2 fusion.12
  8.5 0.0 copy-start.6
  8.6 9.8 %collective-permute-done.1 = bf16[2,2,8,5120]{3,2,1,0:T(8,128)(2,1)S(1)} collective-permute-done((bf16[2,2,8,5120]{3,2,1,0:T(8,128)(2,1)S(1)}, bf16[2,2,8,5120]{3,2,1,0:T(8,128)(2,1)S(1)}, u32[]{:S(2)}, u32[]{:S(2)}) %collective-permute-start.1) | collective-permute-done | bytes 327712 | tf_op jit(solution)/shard_map/ppermute | solution.py:92
  18.5 0.0 copy-start.10
  18.5 0.9 convert_reduce_fusion
  19.4 0.3 fusion.2
  19.8 0.3 fusion.5
  20.1 0.0 copy-start.2
  20.1 20.6 %collective-permute-start.7 = (bf16[64,5120]{1,0:T(8,128)(2,1)S(1)}, bf16[64,5120]{1,0:T(8,128)(2,1)S(1)}, u32[]{:S(2)}, u32[]{:S(2)}) collective-permute-start(bf16[64,5120]{1,0:T(8,128)(2,1)S(1)} %bitcast.30), channel_id=1, source_target_pairs={{0,1},{1,0},{2,3},{3,2},{4,5},{5,4},{6,7},{7,6},{8,9},{9,8},{10,11... | collective-permute-start | bytes 1966088 | tf_op jit(solution)/shard_map/ppermute | solution.py:102
  40.7 4.4 %collective-permute-start.6 = (bf16[64,5120]{1,0:T(8,128)(2,1)S(1)}, bf16[64,5120]{1,0:T(8,128)(2,1)S(1)}, u32[]{:S(2)}, u32[]{:S(2)}) collective-permute-start(bf16[64,5120]{1,0:T(8,128)(2,1)S(1)} %bitcast.32), channel_id=1, source_target_pairs={{0,6},{2,0},{4,2},{6,4},{1,7},{3,1},{5,3},{7,5},{8,14},{10,8},{12,... | collective-permute-start | bytes 1966088 | tf_op jit(solution)/shard_map/ppermute | solution.py:114
  45.1 0.9 convolution_convert_fusion.11.refs_0_
  46.0 0.0 copy-start.4
  46.0 0.9 convolution_convert_fusion.10.refs_1_
  46.8 1.2 %copy-done.4 = bf16[5120,384]{1,0:T(8,128)(2,1)S(1)} copy-done((bf16[5120,384]{1,0:T(8,128)(2,1)S(1)}, bf16[5120,384]{1,0:T(8,128)(2,1)}, u32[]{:S(2)}) %copy-start.4) | copy-done | bytes 3932184
  48.1 0.9 convolution_convert_fusion.9.refs_2_
  48.9 21.5 %collective-permute-done.5 = bf16[64,5120]{1,0:T(8,128)(2,1)S(1)} collective-permute-done((bf16[64,5120]{1,0:T(8,128)(2,1)S(1)}, bf16[64,5120]{1,0:T(8,128)(2,1)S(1)}, u32[]{:S(2)}, u32[]{:S(2)}) %collective-permute-start.5) | collective-permute-done | bytes 655392 | tf_op jit(solution)/shard_map/ppermute | solution.py:113
  70.5 0.8 copy-done.7
  71.2 0.2 copy-done.8
  71.5 1.0 collective-permute-start.10
  72.5 0.1 stack.35.at
  72.6 1.0 slice.44
  73.6 1.0 slice.45
  74.6 4.4 %collective-permute-start.8 = (bf16[32,5120]{1,0:T(8,128)(2,1)S(1)}, bf16[32,5120]{1,0:T(8,128)(2,1)S(1)}, u32[]{:S(2)}, u32[]{:S(2)}) collective-permute-start(bf16[32,5120]{1,0:T(8,128)(2,1)S(1)} %slice.44), channel_id=1, source_target_pairs={{0,2},{2,4},{4,6},{6,0},{1,3},{3,5},{5,7},{7,1},{8,10},{10,12},{12... | collective-permute-start | bytes 983048 | tf_op jit(solution)/shard_map/ppermute | solution.py:118
  79.1 3.0 %convolution_convert_fusion.8.refs_3_ = bf16[128,384]{1,0:T(8,128)(2,1)S(1)} fusion(bf16[128,5120]{1,0:T(8,128)(2,1)S(1)} %constant_dynamic-update-slice_fusion, bf16[5120,384]{1,0:T(8,128)(2,1)} %param.13), kind=kOutput, calls=%fused_computation.20 | convolution fusion | flops 503365632 | bytes 5341184 | tf_op jit(solution)/shard_map/dot_general | solution.py:106
  82.1 0.9 convolution_convert_fusion.7.refs_4_
  83.0 1.2 %copy-done.5 = bf16[5120,384]{1,0:T(8,128)(2,1)S(1)} copy-done((bf16[5120,384]{1,0:T(8,128)(2,1)S(1)}, bf16[5120,384]{1,0:T(8,128)(2,1)}, u32[]{:S(2)}) %copy-start.5) | copy-done | bytes 3932184
  84.2 0.9 convolution_convert_fusion.6.refs_5_
  85.1 1.2 %copy-done.1 = bf16[5120,384]{1,0:T(8,128)(2,1)S(1)} copy-done((bf16[5120,384]{1,0:T(8,128)(2,1)S(1)}, bf16[5120,384]{1,0:T(8,128)(2,1)}, u32[]{:S(2)}) %copy-start.1) | copy-done | bytes 3932184
  86.3 0.9 convolution_convert_fusion.5.refs_6_
  87.2 0.9 convolution_convert_fusion.4.refs_7_
  88.1 0.9 convolution_convert_fusion.3.refs_8_
  89.0 4.0 %collective-permute-done.8 = bf16[32,5120]{1,0:T(8,128)(2,1)S(1)} collective-permute-done((bf16[32,5120]{1,0:T(8,128)(2,1)S(1)}, bf16[32,5120]{1,0:T(8,128)(2,1)S(1)}, u32[]{:S(2)}, u32[]{:S(2)}) %collective-permute-start.8) | collective-permute-done | bytes 327712 | tf_op jit(solution)/shard_map/ppermute | solution.py:118
  93.0 3.1 %collective-permute-done.9 = bf16[32,5120]{1,0:T(8,128)(2,1)S(1)} collective-permute-done((bf16[32,5120]{1,0:T(8,128)(2,1)S(1)}, bf16[32,5120]{1,0:T(8,128)(2,1)S(1)}, u32[]{:S(2)}, u32[]{:S(2)}) %collective-permute-start.9) | collective-permute-done | bytes 327712 | tf_op jit(solution)/shard_map/ppermute | solution.py:118
  96.2 1.1 %collective-permute-start.11 = (bf16[64,5120]{1,0:T(8,128)(2,1)S(1)}, bf16[64,5120]{1,0:T(8,128)(2,1)S(1)}, u32[]{:S(2)}, u32[]{:S(2)}) collective-permute-start(bf16[64,5120]{1,0:T(8,128)(2,1)S(1)} %pad_maximum_fusion.1), channel_id=1, source_target_pairs={{0,1},{1,0},{2,3},{3,2},{4,5},{5,4},{6,7},{7,6},{8,9},{9,8},{10,11... | collective-permute-start | bytes 1966088 | tf_op jit(solution)/shard_map/ppermute | solution.py:102
  97.3 1.7 %collective-permute-done.11 = bf16[64,5120]{1,0:T(8,128)(2,1)S(1)} collective-permute-done((bf16[64,5120]{1,0:T(8,128)(2,1)S(1)}, bf16[64,5120]{1,0:T(8,128)(2,1)S(1)}, u32[]{:S(2)}, u32[]{:S(2)}) %collective-permute-start.11) | collective-permute-done | bytes 655392 | tf_op jit(solution)/shard_map/ppermute | solution.py:102
  99.1 0.9 convolution_convert_fusion.2.refs_9_
  100.0 0.9 convolution_convert_fusion.1.refs_10_
  100.9 0.9 convolution_convert_fusion.refs_11_
  101.8 2.7 %shard_map.82 = bf16[512,384]{1,0:T(8,128)(2,1)} custom-call(s32[8]{0:T(128)S(1)} %stack.35.at, bf16[128,384]{1,0:T(8,128)(2,1)S(1)} %convolution_convert_fusion.11.refs_0_, bf16[128,384]{1,0:T(8,128)(2,1)S(1)} %convolution_convert_fusion.10.refs_1_, bf16[128,384]{1,0:T(8,128)(2,1)S(1)} %convolution_convert_fusion.9.refs_2_, ...), custom_call_target="tpu_custom_call" | custom-call | tf_op jit(solution)/shard_map/pallas_call | solution.py:162
  (40 shorter events, 0.4 us)
Async XLA Ops:
  0.0 7.8 %copy-start.11 = (s32[32,16]{0,1:T(8,128)S(1)}, s32[32,16]{0,1:T(8,128)}, u32[]{:S(2)}) copy-start(s32[32,16]{0,1:T(8,128)} %param.9) | copy-start | bytes 6148
  0.0 8.3 %copy-start.12 = (s32[32,16]{0,1:T(8,128)S(1)}, s32[32,16]{0,1:T(8,128)}, u32[]{:S(2)}) copy-start(s32[32,16]{0,1:T(8,128)} %param.10) | copy-start | bytes 6148
  0.0 8.5 %copy-start.9 = (f32[5120]{0:T(1024)S(1)}, f32[5120]{0:T(1024)}, u32[]{:S(2)}) copy-start(f32[5120]{0:T(1024)} %param.12) | copy-start | bytes 61444
  0.0 18.5 %collective-permute-start.2 = (bf16[2,2,16,5120]{3,2,1,0:T(8,128)(2,1)}, bf16[2,2,16,5120]{3,2,1,0:T(8,128)(2,1)S(1)}, u32[]{:S(2)}, u32[]{:S(2)}) collective-permute-start(bf16[2,2,16,5120]{3,2,1,0:T(8,128)(2,1)} %param.8), channel_id=1, source_target_pairs={{7,32},{32,7},{15,40},{40,15},{23,48},{48,23},{31,56},{56,31},{39,... | collective-permute-start | bytes 1966088 | tf_op jit(solution)/shard_map/ppermute | solution.py:88
  2.0 6.5 %collective-permute-start.3 = (bf16[2,2,8,5120]{3,2,1,0:T(8,128)(2,1)S(1)}, bf16[2,2,8,5120]{3,2,1,0:T(8,128)(2,1)S(1)}, u32[]{:S(2)}, u32[]{:S(2)}) collective-permute-start(bf16[2,2,8,5120]{3,2,1,0:T(8,128)(2,1)S(1)} %get-tuple-element.49), channel_id=1, source_target_pairs={{23,40},{48,15},{15,48},{40,23},{55,72},{80,47},{47,80},{72,55},{8... | collective-permute-start | bytes 983048 | tf_op jit(solution)/shard_map/ppermute | solution.py:89
  2.7 5.9 %collective-permute-start = (bf16[2,2,8,5120]{3,2,1,0:T(8,128)(2,1)S(1)}, bf16[2,2,8,5120]{3,2,1,0:T(8,128)(2,1)S(1)}, u32[]{:S(2)}, u32[]{:S(2)}) collective-permute-start(bf16[2,2,8,5120]{3,2,1,0:T(8,128)(2,1)S(1)} %get-tuple-element.49), channel_id=1, source_target_pairs={{8,16},{16,8},{40,48},{48,40},{9,17},{17,9},{41,49},{49,41},{10,18... | collective-permute-start | bytes 983048 | tf_op jit(solution)/shard_map/ppermute | solution.py:91
  3.4 5.2 %collective-permute-start.4 = (bf16[2,2,8,5120]{3,2,1,0:T(8,128)(2,1)S(1)}, bf16[2,2,8,5120]{3,2,1,0:T(8,128)(2,1)S(1)}, u32[]{:S(2)}, u32[]{:S(2)}) collective-permute-start(bf16[2,2,8,5120]{3,2,1,0:T(8,128)(2,1)S(1)} %get-tuple-element.50), channel_id=1, source_target_pairs={{15,32},{40,7},{7,40},{32,15},{31,48},{56,23},{23,56},{48,31},{47,... | collective-permute-start | bytes 983048 | tf_op jit(solution)/shard_map/ppermute | solution.py:90
  4.1 14.4 %collective-permute-start.1 = (bf16[2,2,8,5120]{3,2,1,0:T(8,128)(2,1)S(1)}, bf16[2,2,8,5120]{3,2,1,0:T(8,128)(2,1)S(1)}, u32[]{:S(2)}, u32[]{:S(2)}) collective-permute-start(bf16[2,2,8,5120]{3,2,1,0:T(8,128)(2,1)S(1)} %get-tuple-element.50), channel_id=1, source_target_pairs={{0,8},{8,0},{1,9},{9,1},{2,10},{10,2},{3,11},{11,3},{4,12},{12,4},... | collective-permute-start | bytes 983048 | tf_op jit(solution)/shard_map/ppermute | solution.py:92
  8.5 10.0 %copy-start.6 = (bf16[2,2,16,5120]{3,2,1,0:T(8,128)(2,1)S(1)}, bf16[2,2,16,5120]{3,2,1,0:T(8,128)(2,1)}, u32[]{:S(2)}) copy-start(bf16[2,2,16,5120]{3,2,1,0:T(8,128)(2,1)} %param.8) | copy-start | bytes 1966084
  18.5 1.3 %copy-start.10 = (f32[5120]{0:T(1024)S(1)}, f32[5120]{0:T(1024)}, u32[]{:S(2)}) copy-start(f32[5120]{0:T(1024)} %param.11) | copy-start | bytes 61444
  18.5 26.6 %copy-start = (bf16[5120,384]{1,0:T(8,128)(2,1)S(1)}, bf16[5120,384]{1,0:T(8,128)(2,1)}, u32[]{:S(2)}) copy-start(bf16[5120,384]{1,0:T(8,128)(2,1)} %param.13) | copy-start | bytes 11796484
  20.1 25.9 %copy-start.2 = (bf16[5120,384]{1,0:T(8,128)(2,1)S(1)}, bf16[5120,384]{1,0:T(8,128)(2,1)}, u32[]{:S(2)}) copy-start(bf16[5120,384]{1,0:T(8,128)(2,1)} %param.14) | copy-start | bytes 11796484
  20.1 25.0 %collective-permute-start.7 = (bf16[64,5120]{1,0:T(8,128)(2,1)S(1)}, bf16[64,5120]{1,0:T(8,128)(2,1)S(1)}, u32[]{:S(2)}, u32[]{:S(2)}) collective-permute-start(bf16[64,5120]{1,0:T(8,128)(2,1)S(1)} %bitcast.30), channel_id=1, source_target_pairs={{0,1},{1,0},{2,3},{3,2},{4,5},{5,4},{6,7},{7,6},{8,9},{9,8},{10,11... | collective-permute-start | bytes 1966088 | tf_op jit(solution)/shard_map/ppermute | solution.py:102
  40.7 29.7 %collective-permute-start.5 = (bf16[64,5120]{1,0:T(8,128)(2,1)S(1)}, bf16[64,5120]{1,0:T(8,128)(2,1)S(1)}, u32[]{:S(2)}, u32[]{:S(2)}) collective-permute-start(bf16[64,5120]{1,0:T(8,128)(2,1)S(1)} %bitcast.31), channel_id=1, source_target_pairs={{0,2},{2,4},{4,6},{6,0},{1,3},{3,5},{5,7},{7,1},{8,10},{10,12},{12... | collective-permute-start | bytes 1966088 | tf_op jit(solution)/shard_map/ppermute | solution.py:113
  40.7 29.7 %collective-permute-start.6 = (bf16[64,5120]{1,0:T(8,128)(2,1)S(1)}, bf16[64,5120]{1,0:T(8,128)(2,1)S(1)}, u32[]{:S(2)}, u32[]{:S(2)}) collective-permute-start(bf16[64,5120]{1,0:T(8,128)(2,1)S(1)} %bitcast.32), channel_id=1, source_target_pairs={{0,6},{2,0},{4,2},{6,4},{1,7},{3,1},{5,3},{7,5},{8,14},{10,8},{12,... | collective-permute-start | bytes 1966088 | tf_op jit(solution)/shard_map/ppermute | solution.py:114
  46.0 2.1 %copy-start.4 = (bf16[5120,384]{1,0:T(8,128)(2,1)S(1)}, bf16[5120,384]{1,0:T(8,128)(2,1)}, u32[]{:S(2)}) copy-start(bf16[5120,384]{1,0:T(8,128)(2,1)} %param.15) | copy-start | bytes 11796484
  70.4 0.8 copy-start.7
  70.4 1.1 %copy-start.8 = (bf16[64,5120]{1,0:T(8,128)(2,1)}, bf16[64,5120]{1,0:T(8,128)(2,1)S(1)}, u32[]{:S(2)}) copy-start(bf16[64,5120]{1,0:T(8,128)(2,1)S(1)} %collective-permute-done.6) | copy-start | bytes 1966084
  71.5 13.6 %collective-permute-start.10 = (bf16[128,5120]{1,0:T(8,128)(2,1)S(1)}, bf16[128,5120]{1,0:T(8,128)(2,1)S(1)}, u32[]{:S(2)}, u32[]{:S(2)}) collective-permute-start(bf16[128,5120]{1,0:T(8,128)(2,1)S(1)} %constant_dynamic-update-slice_fusion), channel_id=1, source_target_pairs={{0,1},{1,0},{2,3},{3,2},{4,5},{5,4},{6,7},{7,6},{8,9},{9,8},{10,11... | collective-permute-start | bytes 3932168 | tf_op jit(solution)/shard_map/ppermute | solution.py:102
  74.6 7.4 %copy-start.3 = (bf16[5120,384]{1,0:T(8,128)(2,1)S(1)}, bf16[5120,384]{1,0:T(8,128)(2,1)}, u32[]{:S(2)}) copy-start(bf16[5120,384]{1,0:T(8,128)(2,1)} %param.14) | copy-start | bytes 11796484
  74.6 18.4 %collective-permute-start.8 = (bf16[32,5120]{1,0:T(8,128)(2,1)S(1)}, bf16[32,5120]{1,0:T(8,128)(2,1)S(1)}, u32[]{:S(2)}, u32[]{:S(2)}) collective-permute-start(bf16[32,5120]{1,0:T(8,128)(2,1)S(1)} %slice.44), channel_id=1, source_target_pairs={{0,2},{2,4},{4,6},{6,0},{1,3},{3,5},{5,7},{7,1},{8,10},{10,12},{12... | collective-permute-start | bytes 983048 | tf_op jit(solution)/shard_map/ppermute | solution.py:118
  79.1 17.1 %collective-permute-start.9 = (bf16[32,5120]{1,0:T(8,128)(2,1)S(1)}, bf16[32,5120]{1,0:T(8,128)(2,1)S(1)}, u32[]{:S(2)}, u32[]{:S(2)}) collective-permute-start(bf16[32,5120]{1,0:T(8,128)(2,1)S(1)} %slice.45), channel_id=1, source_target_pairs={{0,6},{2,0},{4,2},{6,4},{1,7},{3,1},{5,3},{7,5},{8,14},{10,8},{12,... | collective-permute-start | bytes 983048 | tf_op jit(solution)/shard_map/ppermute | solution.py:118
  82.0 2.1 %copy-start.5 = (bf16[5120,384]{1,0:T(8,128)(2,1)S(1)}, bf16[5120,384]{1,0:T(8,128)(2,1)}, u32[]{:S(2)}) copy-start(bf16[5120,384]{1,0:T(8,128)(2,1)} %param.15) | copy-start | bytes 11796484
  84.2 2.1 %copy-start.1 = (bf16[5120,384]{1,0:T(8,128)(2,1)S(1)}, bf16[5120,384]{1,0:T(8,128)(2,1)}, u32[]{:S(2)}) copy-start(bf16[5120,384]{1,0:T(8,128)(2,1)} %param.13) | copy-start | bytes 11796484
  96.2 2.8 %collective-permute-start.11 = (bf16[64,5120]{1,0:T(8,128)(2,1)S(1)}, bf16[64,5120]{1,0:T(8,128)(2,1)S(1)}, u32[]{:S(2)}, u32[]{:S(2)}) collective-permute-start(bf16[64,5120]{1,0:T(8,128)(2,1)S(1)} %pad_maximum_fusion.1), channel_id=1, source_target_pairs={{0,1},{1,0},{2,3},{3,2},{4,5},{5,4},{6,7},{7,6},{8,9},{9,8},{10,11... | collective-permute-start | bytes 1966088 | tf_op jit(solution)/shard_map/ppermute | solution.py:102

commit v3 on v2

--- a/solution.py
+++ b/solution.py
@@ -112,18 +112,19 @@
 
     prev = lax.ppermute(own, "zh", ring(1))
     nxt = lax.ppermute(own, "zh", ring(-1))
-    own_q = weights_on(both_cores(own))
-    prev, nxt, *own_q = lax.optimization_barrier((prev, nxt, *own_q))
+    own_q = weights_on(own)
+    prev, nxt, own_q = lax.optimization_barrier((prev, nxt, own_q))
+    far = [lax.ppermute(prev[:32], "zh", ring(1)), lax.ppermute(nxt[32:], "zh", ring(-1))]
     side = jnp.concatenate([prev, nxt], 0)
-    far = [lax.ppermute(side[:32], "zh", ring(1)), lax.ppermute(side[96:], "zh", ring(-1))]
-    side_q, side_x = weights_on(side), weights_on(core_swap(side))
-    *far, side_q, side_x = lax.optimization_barrier((*far, side_q, side_x))
+    side_q = weights_on(side)
+    near_x = weights_on(core_swap(jnp.concatenate([own, side], 0)))
+    far, side_q, near_x = lax.optimization_barrier((far, side_q, near_x))
     far = jnp.concatenate(far, 0)
     far_q = weights_on(both_cores(far))
     at = [
         (((zh - d) % 4) * 2 + core) * 64 for core in (c, 1 - c) for d in (0, 1, 3, 2)
     ]
-    return attention(jnp.stack(at).astype(jnp.int32), own_q, side_q, side_x, far_q)
+    return attention(jnp.stack(at).astype(jnp.int32), own_q, side_q, near_x, far_q)
 
 
 def attention_kernel(at, *refs):
@@ -133,13 +134,11 @@
         whole[pl.ds(pl.multiple_of(at[n], 64), 64), :] = rows
 
     for n, whole in enumerate(wholes):
-        own, side, side_x, far = parts[n::3]
-        for core, pair in enumerate((side, side_x)):
-            rows = slice(core * 64, core * 64 + 64)
-            put(whole, core * 4, own[rows, :])
-            put(whole, core * 4 + 1, pair[:64, :])
-            put(whole, core * 4 + 2, pair[64:, :])
-            put(whole, core * 4 + 3, far[rows, :])
+        own, side, near_x, far = parts[n::3]
+        blocks = [own[...], side[:64, :], side[64:, :], far[:64, :]]
+        blocks += [near_x[m * 64 : m * 64 + 64, :] for m in range(3)] + [far[64:, :]]
+        for m, rows in enumerate(blocks):
+            put(whole, m, rows)
     q_all, k_all, v_all = wholes
     for h in range(out.shape[1] // HD):
         cols = slice(h * HD, h * HD + HD)

time: 105 us -> 102 us (0.971)
  the two profiles are of different devices: /device:TPU:9 before, /device:TPU:19 now
where the time goes in v3:
time: 102 us
  starting transfers between devices  43.3 us (42%)
  waiting for transfers between devices  38.4 us (38%)
  matrix products  11.2 us (11%)
  other arithmetic  3.46 us (3%)
  Pallas kernels  2.74 us (3%)
  local copies, waits for them, and re-layouts  1.94 us (2%)
    ppermute x1, starting transfers between devices, local(): nxt = lax.ppermute(own, 'zh', ring(-1))  20.2 us
    ppermute x1, waiting for transfers between devices, local(): prev = lax.ppermute(own, 'zh', ring(1))  17.5 us
    dot_general x12, matrix products, weights_on(): jnp.dot(rows, w, preferred_element_type=jnp.float32).astype(jnp.bfloat16)  11.2 us
    ppermute x1, starting transfers between devices, local(): prev = lax.ppermute(own, 'zh', ring(1))  8.02 us
    ppermute x1, waiting for transfers between devices, local(): lax.ppermute(prev[:32], 'zh', ring(1))  6.42 us
    ppermute x1, waiting for transfers between devices, local(): out_other = lax.ppermute(outer, ('x', 'zl'), OUTER_PAIRS)  5.5 us
    ppermute x2, starting transfers between devices, core_swap(): return lax.ppermute(v, 'c', SWAP)  4.63 us
    ppermute x1, starting transfers between devices, local(): lax.ppermute(nxt[32:], 'zh', ring(-1))  4.57 us
  transfers between devices with their start and end apart: 11, of which 7 were waited for; matrix products, arithmetic and copies ran while one was open for 11% of the time, Pallas kernels for 0%

profile of v3, /device:TPU:19, one launch (start us, length us, event | category | flops | bytes accessed | tf_op | source)
XLA Modules:
  0.0 101.6 jit_solution(13447020959307486497)
XLA Ops:
  0.0 0.8 collective-permute-start.2
  0.9 1.1 %broadcast_select_fusion.5 = (bf16[2,2,8,5120]{3,2,1,0:T(8,128)(2,1)S(1)}, bf16[2,2,8,5120]{3,2,1,0:T(8,128)(2,1)S(1)}) fusion(pred[]{:T(512)S(6)} %eq.27, bf16[2,2,16,5120]{3,2,1,0:T(8,128)(2,1)} %param.8), kind=kLoop, calls=%fused_computation.30 | loop fusion | flops 327680 | bytes 1310721 | tf_op jit(solution)/shard_map/jit(_where)/select_n | solution.py:76
  2.0 0.7 collective-permute-start.3
  2.7 3.5 %collective-permute-start = (bf16[2,2,8,5120]{3,2,1,0:T(8,128)(2,1)S(1)}, bf16[2,2,8,5120]{3,2,1,0:T(8,128)(2,1)S(1)}, u32[]{:S(2)}, u32[]{:S(2)}) collective-permute-start(bf16[2,2,8,5120]{3,2,1,0:T(8,128)(2,1)S(1)} %get-tuple-element.49), channel_id=1, source_target_pairs={{8,16},{16,8},{40,48},{48,40},{9,17},{17,9},{41,49},{49,41},{10,18... | collective-permute-start | bytes 983048 | tf_op jit(solution)/shard_map/ppermute | solution.py:91
  6.2 0.7 collective-permute-start.4
  6.9 0.1 collective-permute-start.1
  7.1 0.2 dynamic-slice_reduce_fusion.1
  7.3 0.2 fusion.9
  7.5 0.1 fusion.13
  7.7 0.2 fusion.12
  7.9 0.1 stack.35.at
  8.0 0.0 copy-start.3
  8.0 0.0 collective-permute-done.3
  8.1 5.5 %collective-permute-done = bf16[2,2,8,5120]{3,2,1,0:T(8,128)(2,1)S(1)} collective-permute-done((bf16[2,2,8,5120]{3,2,1,0:T(8,128)(2,1)S(1)}, bf16[2,2,8,5120]{3,2,1,0:T(8,128)(2,1)S(1)}, u32[]{:S(2)}, u32[]{:S(2)}) %collective-permute-start) | collective-permute-done | bytes 327712 | tf_op jit(solution)/shard_map/ppermute | solution.py:91
  13.6 1.1 %collective-permute-done.1 = bf16[2,2,8,5120]{3,2,1,0:T(8,128)(2,1)S(1)} collective-permute-done((bf16[2,2,8,5120]{3,2,1,0:T(8,128)(2,1)S(1)}, bf16[2,2,8,5120]{3,2,1,0:T(8,128)(2,1)S(1)}, u32[]{:S(2)}, u32[]{:S(2)}) %collective-permute-start.1) | collective-permute-done | bytes 327712 | tf_op jit(solution)/shard_map/ppermute | solution.py:92
  14.7 0.0 copy-start.5
  14.7 0.0 copy-start
  14.7 0.9 convert_reduce_fusion
  15.6 0.3 fusion.2
  16.0 0.3 fusion.5
  16.3 0.0 copy-start.1
  16.3 8.0 %collective-permute-start.5 = (bf16[64,5120]{1,0:T(8,128)(2,1)S(1)}, bf16[64,5120]{1,0:T(8,128)(2,1)S(1)}, u32[]{:S(2)}, u32[]{:S(2)}) collective-permute-start(bf16[64,5120]{1,0:T(8,128)(2,1)S(1)} %bitcast.33), channel_id=1, source_target_pairs={{0,2},{2,4},{4,6},{6,0},{1,3},{3,5},{5,7},{7,1},{8,10},{10,12},{12... | collective-permute-start | bytes 1966088 | tf_op jit(solution)/shard_map/ppermute | solution.py:113
  24.3 20.2 %collective-permute-start.6 = (bf16[64,5120]{1,0:T(8,128)(2,1)S(1)}, bf16[64,5120]{1,0:T(8,128)(2,1)S(1)}, u32[]{:S(2)}, u32[]{:S(2)}) collective-permute-start(bf16[64,5120]{1,0:T(8,128)(2,1)S(1)} %bitcast.34), channel_id=1, source_target_pairs={{0,6},{2,0},{4,2},{6,4},{1,7},{3,1},{5,3},{7,5},{8,14},{10,8},{12,... | collective-permute-start | bytes 1966088 | tf_op jit(solution)/shard_map/ppermute | solution.py:114
  44.5 0.7 convolution_convert_fusion.11.refs_0_
  45.2 0.0 copy-start.2
  45.2 0.7 convolution_convert_fusion.10.refs_1_
  45.9 1.4 %copy-done.2 = bf16[5120,384]{1,0:T(8,128)(2,1)S(1)} copy-done((bf16[5120,384]{1,0:T(8,128)(2,1)S(1)}, bf16[5120,384]{1,0:T(8,128)(2,1)}, u32[]{:S(2)}) %copy-start.2) | copy-done | bytes 3932184
  47.3 0.7 convolution_convert_fusion.9.refs_2_
  48.0 17.5 %collective-permute-done.5 = bf16[64,5120]{1,0:T(8,128)(2,1)S(1)} collective-permute-done((bf16[64,5120]{1,0:T(8,128)(2,1)S(1)}, bf16[64,5120]{1,0:T(8,128)(2,1)S(1)}, u32[]{:S(2)}, u32[]{:S(2)}) %collective-permute-start.5) | collective-permute-done | bytes 655392 | tf_op jit(solution)/shard_map/ppermute | solution.py:113
  65.5 4.0 %collective-permute-done.6 = bf16[64,5120]{1,0:T(8,128)(2,1)S(1)} collective-permute-done((bf16[64,5120]{1,0:T(8,128)(2,1)S(1)}, bf16[64,5120]{1,0:T(8,128)(2,1)S(1)}, u32[]{:S(2)}, u32[]{:S(2)}) %collective-permute-start.6) | collective-permute-done | bytes 655392 | tf_op jit(solution)/shard_map/ppermute | solution.py:114
  69.6 0.1 pad_maximum_fusion
  69.7 4.0 %collective-permute-start.9 = (bf16[192,5120]{1,0:T(8,128)(2,1)S(1)}, bf16[192,5120]{1,0:T(8,128)(2,1)S(1)}, u32[]{:S(2)}, u32[]{:S(2)}) collective-permute-start(bf16[192,5120]{1,0:T(8,128)(2,1)S(1)} %pad_maximum_fusion), channel_id=1, source_target_pairs={{0,1},{1,0},{2,3},{3,2},{4,5},{5,4},{6,7},{7,6},{8,9},{9,8},{10,11... | collective-permute-start | bytes 5898248 | tf_op jit(solution)/shard_map/ppermute | solution.py:102
  73.9 0.1 collective-permute-start.7
  74.0 4.6 %collective-permute-start.8 = (bf16[32,5120]{1,0:T(8,128)(2,1)S(1)}, bf16[32,5120]{1,0:T(8,128)(2,1)S(1)}, u32[]{:S(2)}, u32[]{:S(2)}) collective-permute-start(bf16[32,5120]{1,0:T(8,128)(2,1)S(1)} %slice.45), channel_id=1, source_target_pairs={{0,6},{2,0},{4,2},{6,4},{1,7},{3,1},{5,3},{7,5},{8,14},{10,8},{12,... | collective-permute-start | bytes 983048 | tf_op jit(solution)/shard_map/ppermute | solution.py:117
  78.6 0.9 convolution_convert_fusion.8.refs_3_
  79.5 0.9 convolution_convert_fusion.7.refs_4_
  80.4 0.9 convolution_convert_fusion.6.refs_5_
  81.3 1.2 %convolution_convert_fusion.2.refs_6_ = bf16[192,384]{1,0:T(8,128)(2,1)S(1)} fusion(bf16[192,5120]{1,0:T(8,128)(2,1)S(1)} %collective-permute-done.9, bf16[5120,384]{1,0:T(8,128)(2,1)S(1)} %copy-done), kind=kOutput, calls=%fused_computation.14 | convolution fusion | flops 755048448 | bytes 6045696 | tf_op jit(solution)/shard_map/dot_general | solution.py:106
  82.6 1.2 %convolution_convert_fusion.1.refs_7_ = bf16[192,384]{1,0:T(8,128)(2,1)S(1)} fusion(bf16[192,5120]{1,0:T(8,128)(2,1)S(1)} %collective-permute-done.9, bf16[5120,384]{1,0:T(8,128)(2,1)S(1)} %copy-done.1), kind=kOutput, calls=%fused_computation.13 | convolution fusion | flops 755048448 | bytes 6045696 | tf_op jit(solution)/shard_map/dot_general | solution.py:106
  83.8 1.2 %convolution_convert_fusion.refs_8_ = bf16[192,384]{1,0:T(8,128)(2,1)S(1)} fusion(bf16[192,5120]{1,0:T(8,128)(2,1)S(1)} %collective-permute-done.9, bf16[5120,384]{1,0:T(8,128)(2,1)S(1)} %copy-done.2), kind=kOutput, calls=%fused_computation.12 | convolution fusion | flops 755048448 | bytes 6045696 | tf_op jit(solution)/shard_map/dot_general | solution.py:106
  85.1 6.4 %collective-permute-done.7 = bf16[32,5120]{1,0:T(8,128)(2,1)S(1)} collective-permute-done((bf16[32,5120]{1,0:T(8,128)(2,1)S(1)}, bf16[32,5120]{1,0:T(8,128)(2,1)S(1)}, u32[]{:S(2)}, u32[]{:S(2)}) %collective-permute-start.7) | collective-permute-done | bytes 327712 | tf_op jit(solution)/shard_map/ppermute | solution.py:117
  91.5 2.2 %collective-permute-done.8 = bf16[32,5120]{1,0:T(8,128)(2,1)S(1)} collective-permute-done((bf16[32,5120]{1,0:T(8,128)(2,1)S(1)}, bf16[32,5120]{1,0:T(8,128)(2,1)S(1)}, u32[]{:S(2)}, u32[]{:S(2)}) %collective-permute-start.8) | collective-permute-done | bytes 327712 | tf_op jit(solution)/shard_map/ppermute | solution.py:117
  93.8 0.6 collective-permute-start.10
  94.4 1.7 %collective-permute-done.10 = bf16[64,5120]{1,0:T(8,128)(2,1)S(1)} collective-permute-done((bf16[64,5120]{1,0:T(8,128)(2,1)S(1)}, bf16[64,5120]{1,0:T(8,128)(2,1)S(1)}, u32[]{:S(2)}, u32[]{:S(2)}) %collective-permute-start.10) | collective-permute-done | bytes 655392 | tf_op jit(solution)/shard_map/ppermute | solution.py:102
  96.1 0.9 convolution_convert_fusion.5.refs_9_
  97.0 0.9 convolution_convert_fusion.4.refs_10_
  97.9 0.9 convolution_convert_fusion.3.refs_11_
  98.9 2.7 %shard_map.82 = bf16[512,384]{1,0:T(8,128)(2,1)} custom-call(s32[8]{0:T(128)S(1)} %stack.35.at, bf16[64,384]{1,0:T(8,128)(2,1)S(1)} %convolution_convert_fusion.11.refs_0_, bf16[64,384]{1,0:T(8,128)(2,1)S(1)} %convolution_convert_fusion.10.refs_1_, bf16[64,384]{1,0:T(8,128)(2,1)S(1)} %convolution_convert_fusion.9.refs_2_, ...), custom_call_target="tpu_custom_call" | custom-call | tf_op jit(solution)/shard_map/pallas_call | solution.py:161
  (29 shorter events, 0.4 us)
Async XLA Ops:
  0.0 7.0 %copy-start.6 = (s32[32,16]{0,1:T(8,128)S(1)}, s32[32,16]{0,1:T(8,128)}, u32[]{:S(2)}) copy-start(s32[32,16]{0,1:T(8,128)} %param.9) | copy-start | bytes 6148
  0.0 7.6 %copy-start.7 = (s32[32,16]{0,1:T(8,128)S(1)}, s32[32,16]{0,1:T(8,128)}, u32[]{:S(2)}) copy-start(s32[32,16]{0,1:T(8,128)} %param.10) | copy-start | bytes 6148
  0.0 8.0 %copy-start.4 = (f32[5120]{0:T(1024)S(1)}, f32[5120]{0:T(1024)}, u32[]{:S(2)}) copy-start(f32[5120]{0:T(1024)} %param.12) | copy-start | bytes 61444
  0.0 14.7 %collective-permute-start.2 = (bf16[2,2,16,5120]{3,2,1,0:T(8,128)(2,1)}, bf16[2,2,16,5120]{3,2,1,0:T(8,128)(2,1)S(1)}, u32[]{:S(2)}, u32[]{:S(2)}) collective-permute-start(bf16[2,2,16,5120]{3,2,1,0:T(8,128)(2,1)} %param.8), channel_id=1, source_target_pairs={{7,32},{32,7},{15,40},{40,15},{23,48},{48,23},{31,56},{56,31},{39,... | collective-permute-start | bytes 1966088 | tf_op jit(solution)/shard_map/ppermute | solution.py:88
  2.0 6.0 %collective-permute-start.3 = (bf16[2,2,8,5120]{3,2,1,0:T(8,128)(2,1)S(1)}, bf16[2,2,8,5120]{3,2,1,0:T(8,128)(2,1)S(1)}, u32[]{:S(2)}, u32[]{:S(2)}) collective-permute-start(bf16[2,2,8,5120]{3,2,1,0:T(8,128)(2,1)S(1)} %get-tuple-element.49), channel_id=1, source_target_pairs={{23,40},{48,15},{15,48},{40,23},{55,72},{80,47},{47,80},{72,55},{8... | collective-permute-start | bytes 983048 | tf_op jit(solution)/shard_map/ppermute | solution.py:89
  2.7 10.9 %collective-permute-start = (bf16[2,2,8,5120]{3,2,1,0:T(8,128)(2,1)S(1)}, bf16[2,2,8,5120]{3,2,1,0:T(8,128)(2,1)S(1)}, u32[]{:S(2)}, u32[]{:S(2)}) collective-permute-start(bf16[2,2,8,5120]{3,2,1,0:T(8,128)(2,1)S(1)} %get-tuple-element.49), channel_id=1, source_target_pairs={{8,16},{16,8},{40,48},{48,40},{9,17},{17,9},{41,49},{49,41},{10,18... | collective-permute-start | bytes 983048 | tf_op jit(solution)/shard_map/ppermute | solution.py:91
  6.2 1.8 %collective-permute-start.4 = (bf16[2,2,8,5120]{3,2,1,0:T(8,128)(2,1)S(1)}, bf16[2,2,8,5120]{3,2,1,0:T(8,128)(2,1)S(1)}, u32[]{:S(2)}, u32[]{:S(2)}) collective-permute-start(bf16[2,2,8,5120]{3,2,1,0:T(8,128)(2,1)S(1)} %get-tuple-element.50), channel_id=1, source_target_pairs={{15,32},{40,7},{7,40},{32,15},{31,48},{56,23},{23,56},{48,31},{47,... | collective-permute-start | bytes 983048 | tf_op jit(solution)/shard_map/ppermute | solution.py:90
  6.9 7.7 %collective-permute-start.1 = (bf16[2,2,8,5120]{3,2,1,0:T(8,128)(2,1)S(1)}, bf16[2,2,8,5120]{3,2,1,0:T(8,128)(2,1)S(1)}, u32[]{:S(2)}, u32[]{:S(2)}) collective-permute-start(bf16[2,2,8,5120]{3,2,1,0:T(8,128)(2,1)S(1)} %get-tuple-element.50), channel_id=1, source_target_pairs={{0,8},{8,0},{1,9},{9,1},{2,10},{10,2},{3,11},{11,3},{4,12},{12,4},... | collective-permute-start | bytes 983048 | tf_op jit(solution)/shard_map/ppermute | solution.py:92
  8.0 6.7 %copy-start.3 = (bf16[2,2,16,5120]{3,2,1,0:T(8,128)(2,1)S(1)}, bf16[2,2,16,5120]{3,2,1,0:T(8,128)(2,1)}, u32[]{:S(2)}) copy-start(bf16[2,2,16,5120]{3,2,1,0:T(8,128)(2,1)} %param.8) | copy-start | bytes 1966084
  14.7 1.3 %copy-start.5 = (f32[5120]{0:T(1024)S(1)}, f32[5120]{0:T(1024)}, u32[]{:S(2)}) copy-start(f32[5120]{0:T(1024)} %param.11) | copy-start | bytes 61444
  14.7 29.8 %copy-start = (bf16[5120,384]{1,0:T(8,128)(2,1)S(1)}, bf16[5120,384]{1,0:T(8,128)(2,1)}, u32[]{:S(2)}) copy-start(bf16[5120,384]{1,0:T(8,128)(2,1)} %param.13) | copy-start | bytes 11796484
  16.3 28.9 %copy-start.1 = (bf16[5120,384]{1,0:T(8,128)(2,1)S(1)}, bf16[5120,384]{1,0:T(8,128)(2,1)}, u32[]{:S(2)}) copy-start(bf16[5120,384]{1,0:T(8,128)(2,1)} %param.14) | copy-start | bytes 11796484
  16.3 49.2 %collective-permute-start.5 = (bf16[64,5120]{1,0:T(8,128)(2,1)S(1)}, bf16[64,5120]{1,0:T(8,128)(2,1)S(1)}, u32[]{:S(2)}, u32[]{:S(2)}) collective-permute-start(bf16[64,5120]{1,0:T(8,128)(2,1)S(1)} %bitcast.33), channel_id=1, source_target_pairs={{0,2},{2,4},{4,6},{6,0},{1,3},{3,5},{5,7},{7,1},{8,10},{10,12},{12... | collective-permute-start | bytes 1966088 | tf_op jit(solution)/shard_map/ppermute | solution.py:113
  24.3 45.3 %collective-permute-start.6 = (bf16[64,5120]{1,0:T(8,128)(2,1)S(1)}, bf16[64,5120]{1,0:T(8,128)(2,1)S(1)}, u32[]{:S(2)}, u32[]{:S(2)}) collective-permute-start(bf16[64,5120]{1,0:T(8,128)(2,1)S(1)} %bitcast.34), channel_id=1, source_target_pairs={{0,6},{2,0},{4,2},{6,4},{1,7},{3,1},{5,3},{7,5},{8,14},{10,8},{12,... | collective-permute-start | bytes 1966088 | tf_op jit(solution)/shard_map/ppermute | solution.py:114
  45.2 2.1 %copy-start.2 = (bf16[5120,384]{1,0:T(8,128)(2,1)S(1)}, bf16[5120,384]{1,0:T(8,128)(2,1)}, u32[]{:S(2)}) copy-start(bf16[5120,384]{1,0:T(8,128)(2,1)} %param.15) | copy-start | bytes 11796484
  69.7 11.6 %collective-permute-start.9 = (bf16[192,5120]{1,0:T(8,128)(2,1)S(1)}, bf16[192,5120]{1,0:T(8,128)(2,1)S(1)}, u32[]{:S(2)}, u32[]{:S(2)}) collective-permute-start(bf16[192,5120]{1,0:T(8,128)(2,1)S(1)} %pad_maximum_fusion), channel_id=1, source_target_pairs={{0,1},{1,0},{2,3},{3,2},{4,5},{5,4},{6,7},{7,6},{8,9},{9,8},{10,11... | collective-permute-start | bytes 5898248 | tf_op jit(solution)/shard_map/ppermute | solution.py:102
  73.9 17.6 %collective-permute-start.7 = (bf16[32,5120]{1,0:T(8,128)(2,1)S(1)}, bf16[32,5120]{1,0:T(8,128)(2,1)S(1)}, u32[]{:S(2)}, u32[]{:S(2)}) collective-permute-start(bf16[32,5120]{1,0:T(8,128)(2,1)S(1)} %slice.44), channel_id=1, source_target_pairs={{0,2},{2,4},{4,6},{6,0},{1,3},{3,5},{5,7},{7,1},{8,10},{10,12},{12... | collective-permute-start | bytes 983048 | tf_op jit(solution)/shard_map/ppermute | solution.py:117
  74.0 19.7 %collective-permute-start.8 = (bf16[32,5120]{1,0:T(8,128)(2,1)S(1)}, bf16[32,5120]{1,0:T(8,128)(2,1)S(1)}, u32[]{:S(2)}, u32[]{:S(2)}) collective-permute-start(bf16[32,5120]{1,0:T(8,128)(2,1)S(1)} %slice.45), channel_id=1, source_target_pairs={{0,6},{2,0},{4,2},{6,4},{1,7},{3,1},{5,3},{7,5},{8,14},{10,8},{12,... | collective-permute-start | bytes 983048 | tf_op jit(solution)/shard_map/ppermute | solution.py:117
  93.8 2.3 %collective-permute-start.10 = (bf16[64,5120]{1,0:T(8,128)(2,1)S(1)}, bf16[64,5120]{1,0:T(8,128)(2,1)S(1)}, u32[]{:S(2)}, u32[]{:S(2)}) collective-permute-start(bf16[64,5120]{1,0:T(8,128)(2,1)S(1)} %pad_maximum_fusion.1), channel_id=1, source_target_pairs={{0,1},{1,0},{2,3},{3,2},{4,5},{5,4},{6,7},{7,6},{8,9},{9,8},{10,11... | collective-permute-start | bytes 1966088 | tf_op jit(solution)/shard_map/ppermute | solution.py:102

commit v4 on v3

--- a/solution.py
+++ b/solution.py
@@ -90,6 +90,9 @@
     far_inner = lax.ppermute(inner, AX, row_pairs(inner_of))
     out_other = lax.ppermute(outer, ("x", "zl"), OUTER_PAIRS)
     in_other = lax.ppermute(inner, "zl", SWAP)
+    far_rows, far_outer, far_inner, out_other, in_other = lax.optimization_barrier(
+        (far_rows, far_outer, far_inner, out_other, in_other)
+    )
     own = col_mix(tile, latent_rows, out_other, in_other)
     other = col_mix(partner, far_rows, far_outer, far_inner)
     own_r = lax.dynamic_slice(take_row(row_all, tile), (4 * zh + 2 * c,), (OH,))
@@ -110,11 +113,16 @@
     def both_cores(v):
         return jnp.concatenate([v, core_swap(v)], 0)
 
-    prev = lax.ppermute(own, "zh", ring(1))
-    nxt = lax.ppermute(own, "zh", ring(-1))
+    prev_a = lax.ppermute(own[:32], "zh", ring(1))
+    nxt_b = lax.ppermute(own[32:], "zh", ring(-1))
+    prev_b = lax.ppermute(own[32:], "zh", ring(1))
+    nxt_a = lax.ppermute(own[:32], "zh", ring(-1))
     own_q = weights_on(own)
-    prev, nxt, own_q = lax.optimization_barrier((prev, nxt, own_q))
-    far = [lax.ppermute(prev[:32], "zh", ring(1)), lax.ppermute(nxt[32:], "zh", ring(-1))]
+    far = [lax.ppermute(prev_a, "zh", ring(1)), lax.ppermute(nxt_b, "zh", ring(-1))]
+    prev_b, nxt_a, own_q = lax.optimization_barrier((prev_b, nxt_a, own_q))
+    prev, nxt = lax.optimization_barrier(
+        (jnp.concatenate([prev_a, prev_b], 0), jnp.concatenate([nxt_a, nxt_b], 0))
+    )
     side = jnp.concatenate([prev, nxt], 0)
     side_q = weights_on(side)
     near_x = weights_on(core_swap(jnp.concatenate([own, side], 0)))

time: 102 us -> 101 us (level)
  the two profiles are of different devices: /device:TPU:19 before, /device:TPU:61 now
where the time goes in v4:
time: 101 us
  waiting for transfers between devices  41.7 us (41%)
  starting transfers between devices  37.4 us (37%)
  matrix products  11.2 us (11%)
  other arithmetic  3.54 us (4%)
  local copies, waits for them, and re-layouts  3.36 us (3%)
  Pallas kernels  2.74 us (3%)
    ppermute x1, starting transfers between devices, local(): nxt_a = lax.ppermute(own[:32], 'zh', ring(-1))  22.2 us
    ppermute x1, waiting for transfers between devices, local(): prev_b = lax.ppermute(own[32:], 'zh', ring(1))  22.2 us
    dot_general x12, matrix products, weights_on(): jnp.dot(rows, w, preferred_element_type=jnp.float32).astype(jnp.bfloat16)  11.2 us
    ppermute x1, waiting for transfers between devices, local(): lax.ppermute(prev_a, 'zh', ring(1))  8.07 us
    ppermute x1, waiting for transfers between devices, local(): in_other = lax.ppermute(inner, 'zl', SWAP)  4.97 us
    ppermute x1, waiting for transfers between devices, local(): out_other = lax.ppermute(outer, ('x', 'zl'), OUTER_PAIRS)  4.84 us
    ppermute x1, starting transfers between devices, local(): nxt_b = lax.ppermute(own[32:], 'zh', ring(-1))  3.6 us
    ppermute x1, starting transfers between devices, local(): lax.ppermute(nxt_b, 'zh', ring(-1))  3.56 us
  transfers between devices with their start and end apart: 13, of which 5 were waited for; matrix products, arithmetic and copies ran while one was open for 11% of the time, Pallas kernels for 0%

profile of v4, /device:TPU:61, one launch (start us, length us, event | category | flops | bytes accessed | tf_op | source)
XLA Modules:
  0.0 100.5 jit_solution(6217364556088407976)
XLA Ops:
  0.0 0.8 collective-permute-start
  0.9 1.1 %broadcast_select_fusion.4 = (bf16[2,2,8,5120]{3,2,1,0:T(8,128)(2,1)S(1)}, bf16[2,2,8,5120]{3,2,1,0:T(8,128)(2,1)S(1)}) fusion(pred[]{:T(512)S(6)} %eq.27, bf16[2,2,16,5120]{3,2,1,0:T(8,128)(2,1)} %param.8), kind=kLoop, calls=%fused_computation.31 | loop fusion | flops 327680 | bytes 1310721 | tf_op jit(solution)/shard_map/jit(_where)/select_n | solution.py:77
  2.0 0.7 collective-permute-start.1
  2.7 2.4 %collective-permute-start.3 = (bf16[2,2,8,5120]{3,2,1,0:T(8,128)(2,1)S(1)}, bf16[2,2,8,5120]{3,2,1,0:T(8,128)(2,1)S(1)}, u32[]{:S(2)}, u32[]{:S(2)}) collective-permute-start(bf16[2,2,8,5120]{3,2,1,0:T(8,128)(2,1)S(1)} %get-tuple-element.66), channel_id=1, source_target_pairs={{8,16},{16,8},{40,48},{48,40},{9,17},{17,9},{41,49},{49,41},{10,18... | collective-permute-start | bytes 983048 | tf_op jit(solution)/shard_map/ppermute | solution.py:91
  5.1 0.7 collective-permute-start.2
  5.7 0.1 collective-permute-start.4
  5.9 0.2 dynamic-slice_reduce_fusion.1
  6.1 0.2 fusion.9
  6.3 0.1 fusion.13
  6.5 0.2 fusion.12
  6.7 0.1 stack.35.at
  6.8 0.0 copy-start.3
  6.8 0.0 collective-permute-done.1
  6.8 0.0 collective-permute-done.2
  6.9 4.8 %collective-permute-done.3 = bf16[2,2,8,5120]{3,2,1,0:T(8,128)(2,1)S(1)} collective-permute-done((bf16[2,2,8,5120]{3,2,1,0:T(8,128)(2,1)S(1)}, bf16[2,2,8,5120]{3,2,1,0:T(8,128)(2,1)S(1)}, u32[]{:S(2)}, u32[]{:S(2)}) %collective-permute-start.3) | collective-permute-done | bytes 327712 | tf_op jit(solution)/shard_map/ppermute | solution.py:91
  11.7 5.0 %collective-permute-done.4 = bf16[2,2,8,5120]{3,2,1,0:T(8,128)(2,1)S(1)} collective-permute-done((bf16[2,2,8,5120]{3,2,1,0:T(8,128)(2,1)S(1)}, bf16[2,2,8,5120]{3,2,1,0:T(8,128)(2,1)S(1)}, u32[]{:S(2)}, u32[]{:S(2)}) %collective-permute-start.4) | collective-permute-done | bytes 327712 | tf_op jit(solution)/shard_map/ppermute | solution.py:92
  16.7 0.1 broadcast_select_fusion.1
  16.8 0.0 copy-start.5
  16.8 0.0 copy-start
  16.8 0.9 convert_reduce_fusion
  17.7 0.3 fusion.2
  18.0 0.3 fusion.5
  18.4 22.2 %collective-permute-start.6 = (bf16[32,5120]{1,0:T(8,128)(2,1)S(1)}, bf16[32,5120]{1,0:T(8,128)(2,1)S(1)}, u32[]{:S(2)}, u32[]{:S(2)}) collective-permute-start(bf16[32,5120]{1,0:T(8,128)(2,1)S(1)} %bitcast.41), channel_id=1, source_target_pairs={{0,6},{2,0},{4,2},{6,4},{1,7},{3,1},{5,3},{7,5},{8,14},{10,8},{12,... | collective-permute-start | bytes 983048 | tf_op jit(solution)/shard_map/ppermute | solution.py:119
  40.7 0.0 collective-permute-start.7
  40.7 3.6 %collective-permute-start.9 = (bf16[32,5120]{1,0:T(8,128)(2,1)S(1)}, bf16[32,5120]{1,0:T(8,128)(2,1)S(1)}, u32[]{:S(2)}, u32[]{:S(2)}) collective-permute-start(bf16[32,5120]{1,0:T(8,128)(2,1)S(1)} %bitcast.40), channel_id=1, source_target_pairs={{0,6},{2,0},{4,2},{6,4},{1,7},{3,1},{5,3},{7,5},{8,14},{10,8},{12,... | collective-permute-start | bytes 983048 | tf_op jit(solution)/shard_map/ppermute | solution.py:117
  44.3 0.7 convolution_convert_fusion.11.refs_0_
  45.0 1.4 %copy-done.1 = bf16[5120,384]{1,0:T(8,128)(2,1)S(1)} copy-done((bf16[5120,384]{1,0:T(8,128)(2,1)S(1)}, bf16[5120,384]{1,0:T(8,128)(2,1)}, u32[]{:S(2)}) %copy-start.1) | copy-done | bytes 3932184
  46.4 0.7 convolution_convert_fusion.10.refs_1_
  47.1 1.4 %copy-done.2 = bf16[5120,384]{1,0:T(8,128)(2,1)S(1)} copy-done((bf16[5120,384]{1,0:T(8,128)(2,1)S(1)}, bf16[5120,384]{1,0:T(8,128)(2,1)}, u32[]{:S(2)}) %copy-start.2) | copy-done | bytes 3932184
  48.5 0.7 convolution_convert_fusion.9.refs_2_
  49.2 22.2 %collective-permute-done.5 = bf16[32,5120]{1,0:T(8,128)(2,1)S(1)} collective-permute-done((bf16[32,5120]{1,0:T(8,128)(2,1)S(1)}, bf16[32,5120]{1,0:T(8,128)(2,1)S(1)}, u32[]{:S(2)}, u32[]{:S(2)}) %collective-permute-start.5) | collective-permute-done | bytes 327712 | tf_op jit(solution)/shard_map/ppermute | solution.py:118
  71.5 0.1 pad_maximum_fusion
  71.6 2.7 %collective-permute-start.11 = (bf16[192,5120]{1,0:T(8,128)(2,1)S(1)}, bf16[192,5120]{1,0:T(8,128)(2,1)S(1)}, u32[]{:S(2)}, u32[]{:S(2)}) collective-permute-start(bf16[192,5120]{1,0:T(8,128)(2,1)S(1)} %pad_maximum_fusion), channel_id=1, source_target_pairs={{0,1},{1,0},{2,3},{3,2},{4,5},{5,4},{6,7},{7,6},{8,9},{9,8},{10,11... | collective-permute-start | bytes 5898248 | tf_op jit(solution)/shard_map/ppermute | solution.py:105
  74.4 0.1 collective-permute-start.8
  74.5 3.6 %collective-permute-start.10 = (bf16[32,5120]{1,0:T(8,128)(2,1)S(1)}, bf16[32,5120]{1,0:T(8,128)(2,1)S(1)}, u32[]{:S(2)}, u32[]{:S(2)}) collective-permute-start(bf16[32,5120]{1,0:T(8,128)(2,1)S(1)} %collective-permute-done.9), channel_id=1, source_target_pairs={{0,6},{2,0},{4,2},{6,4},{1,7},{3,1},{5,3},{7,5},{8,14},{10,8},{12,... | collective-permute-start | bytes 983048 | tf_op jit(solution)/shard_map/ppermute | solution.py:121
  78.1 0.9 convolution_convert_fusion.8.refs_3_
  79.0 0.9 convolution_convert_fusion.7.refs_4_
  79.9 0.9 convolution_convert_fusion.6.refs_5_
  80.8 1.3 %convolution_convert_fusion.2.refs_6_ = bf16[192,384]{1,0:T(8,128)(2,1)S(1)} fusion(bf16[192,5120]{1,0:T(8,128)(2,1)S(1)} %collective-permute-done.11, bf16[5120,384]{1,0:T(8,128)(2,1)S(1)} %copy-done), kind=kOutput, calls=%fused_computation.14 | convolution fusion | flops 755048448 | bytes 6045696 | tf_op jit(solution)/shard_map/dot_general | solution.py:109
  82.1 1.3 %convolution_convert_fusion.1.refs_7_ = bf16[192,384]{1,0:T(8,128)(2,1)S(1)} fusion(bf16[192,5120]{1,0:T(8,128)(2,1)S(1)} %collective-permute-done.11, bf16[5120,384]{1,0:T(8,128)(2,1)S(1)} %copy-done.1), kind=kOutput, calls=%fused_computation.13 | convolution fusion | flops 755048448 | bytes 6045696 | tf_op jit(solution)/shard_map/dot_general | solution.py:109
  83.4 1.2 %convolution_convert_fusion.refs_8_ = bf16[192,384]{1,0:T(8,128)(2,1)S(1)} fusion(bf16[192,5120]{1,0:T(8,128)(2,1)S(1)} %collective-permute-done.11, bf16[5120,384]{1,0:T(8,128)(2,1)S(1)} %copy-done.2), kind=kOutput, calls=%fused_computation.12 | convolution fusion | flops 755048448 | bytes 6045696 | tf_op jit(solution)/shard_map/dot_general | solution.py:109
  84.6 8.1 %collective-permute-done.8 = bf16[32,5120]{1,0:T(8,128)(2,1)S(1)} collective-permute-done((bf16[32,5120]{1,0:T(8,128)(2,1)S(1)}, bf16[32,5120]{1,0:T(8,128)(2,1)S(1)}, u32[]{:S(2)}, u32[]{:S(2)}) %collective-permute-start.8) | collective-permute-done | bytes 327712 | tf_op jit(solution)/shard_map/ppermute | solution.py:121
  92.7 0.5 collective-permute-start.12
  93.3 1.7 %collective-permute-done.12 = bf16[64,5120]{1,0:T(8,128)(2,1)S(1)} collective-permute-done((bf16[64,5120]{1,0:T(8,128)(2,1)S(1)}, bf16[64,5120]{1,0:T(8,128)(2,1)S(1)}, u32[]{:S(2)}, u32[]{:S(2)}) %collective-permute-start.12) | collective-permute-done | bytes 655392 | tf_op jit(solution)/shard_map/ppermute | solution.py:105
  95.0 0.9 convolution_convert_fusion.5.refs_9_
  95.9 0.9 convolution_convert_fusion.4.refs_10_
  96.9 0.9 convolution_convert_fusion.3.refs_11_
  97.8 2.7 %shard_map.82 = bf16[512,384]{1,0:T(8,128)(2,1)} custom-call(s32[8]{0:T(128)S(1)} %stack.35.at, bf16[64,384]{1,0:T(8,128)(2,1)S(1)} %convolution_convert_fusion.11.refs_0_, bf16[64,384]{1,0:T(8,128)(2,1)S(1)} %convolution_convert_fusion.10.refs_1_, bf16[64,384]{1,0:T(8,128)(2,1)S(1)} %convolution_convert_fusion.9.refs_2_, ...), custom_call_target="tpu_custom_call" | custom-call | tf_op jit(solution)/shard_map/pallas_call | solution.py:169
  (33 shorter events, 0.4 us)
Async XLA Ops:
  0.0 5.9 %copy-start.6 = (s32[32,16]{0,1:T(8,128)S(1)}, s32[32,16]{0,1:T(8,128)}, u32[]{:S(2)}) copy-start(s32[32,16]{0,1:T(8,128)} %param.9) | copy-start | bytes 6148
  0.0 6.5 %copy-start.7 = (s32[32,16]{0,1:T(8,128)S(1)}, s32[32,16]{0,1:T(8,128)}, u32[]{:S(2)}) copy-start(s32[32,16]{0,1:T(8,128)} %param.10) | copy-start | bytes 6148
  0.0 6.8 %copy-start.4 = (f32[5120]{0:T(1024)S(1)}, f32[5120]{0:T(1024)}, u32[]{:S(2)}) copy-start(f32[5120]{0:T(1024)} %param.12) | copy-start | bytes 61444
  0.0 16.7 %collective-permute-start = (bf16[2,2,16,5120]{3,2,1,0:T(8,128)(2,1)}, bf16[2,2,16,5120]{3,2,1,0:T(8,128)(2,1)S(1)}, u32[]{:S(2)}, u32[]{:S(2)}) collective-permute-start(bf16[2,2,16,5120]{3,2,1,0:T(8,128)(2,1)} %param.8), channel_id=1, source_target_pairs={{7,32},{32,7},{15,40},{40,15},{23,48},{48,23},{31,56},{56,31},{39,... | collective-permute-start | bytes 1966088 | tf_op jit(solution)/shard_map/ppermute | solution.py:88
  2.0 4.8 %collective-permute-start.1 = (bf16[2,2,8,5120]{3,2,1,0:T(8,128)(2,1)S(1)}, bf16[2,2,8,5120]{3,2,1,0:T(8,128)(2,1)S(1)}, u32[]{:S(2)}, u32[]{:S(2)}) collective-permute-start(bf16[2,2,8,5120]{3,2,1,0:T(8,128)(2,1)S(1)} %get-tuple-element.66), channel_id=1, source_target_pairs={{23,40},{48,15},{15,48},{40,23},{55,72},{80,47},{47,80},{72,55},{8... | collective-permute-start | bytes 983048 | tf_op jit(solution)/shard_map/ppermute | solution.py:89
  2.7 9.0 %collective-permute-start.3 = (bf16[2,2,8,5120]{3,2,1,0:T(8,128)(2,1)S(1)}, bf16[2,2,8,5120]{3,2,1,0:T(8,128)(2,1)S(1)}, u32[]{:S(2)}, u32[]{:S(2)}) collective-permute-start(bf16[2,2,8,5120]{3,2,1,0:T(8,128)(2,1)S(1)} %get-tuple-element.66), channel_id=1, source_target_pairs={{8,16},{16,8},{40,48},{48,40},{9,17},{17,9},{41,49},{49,41},{10,18... | collective-permute-start | bytes 983048 | tf_op jit(solution)/shard_map/ppermute | solution.py:91
  5.1 1.8 %collective-permute-start.2 = (bf16[2,2,8,5120]{3,2,1,0:T(8,128)(2,1)S(1)}, bf16[2,2,8,5120]{3,2,1,0:T(8,128)(2,1)S(1)}, u32[]{:S(2)}, u32[]{:S(2)}) collective-permute-start(bf16[2,2,8,5120]{3,2,1,0:T(8,128)(2,1)S(1)} %get-tuple-element.65), channel_id=1, source_target_pairs={{15,32},{40,7},{7,40},{32,15},{31,48},{56,23},{23,56},{48,31},{47,... | collective-permute-start | bytes 983048 | tf_op jit(solution)/shard_map/ppermute | solution.py:90
  5.7 10.9 %collective-permute-start.4 = (bf16[2,2,8,5120]{3,2,1,0:T(8,128)(2,1)S(1)}, bf16[2,2,8,5120]{3,2,1,0:T(8,128)(2,1)S(1)}, u32[]{:S(2)}, u32[]{:S(2)}) collective-permute-start(bf16[2,2,8,5120]{3,2,1,0:T(8,128)(2,1)S(1)} %get-tuple-element.65), channel_id=1, source_target_pairs={{0,8},{8,0},{1,9},{9,1},{2,10},{10,2},{3,11},{11,3},{4,12},{12,4},... | collective-permute-start | bytes 983048 | tf_op jit(solution)/shard_map/ppermute | solution.py:92
  6.8 9.9 %copy-start.3 = (bf16[2,2,16,5120]{3,2,1,0:T(8,128)(2,1)S(1)}, bf16[2,2,16,5120]{3,2,1,0:T(8,128)(2,1)}, u32[]{:S(2)}) copy-start(bf16[2,2,16,5120]{3,2,1,0:T(8,128)(2,1)} %param.8) | copy-start | bytes 1966084
  16.8 1.3 %copy-start.5 = (f32[5120]{0:T(1024)S(1)}, f32[5120]{0:T(1024)}, u32[]{:S(2)}) copy-start(f32[5120]{0:T(1024)} %param.11) | copy-start | bytes 61444
  16.8 27.5 %copy-start = (bf16[5120,384]{1,0:T(8,128)(2,1)S(1)}, bf16[5120,384]{1,0:T(8,128)(2,1)}, u32[]{:S(2)}) copy-start(bf16[5120,384]{1,0:T(8,128)(2,1)} %param.13) | copy-start | bytes 11796484
  18.4 53.0 %collective-permute-start.6 = (bf16[32,5120]{1,0:T(8,128)(2,1)S(1)}, bf16[32,5120]{1,0:T(8,128)(2,1)S(1)}, u32[]{:S(2)}, u32[]{:S(2)}) collective-permute-start(bf16[32,5120]{1,0:T(8,128)(2,1)S(1)} %bitcast.41), channel_id=1, source_target_pairs={{0,6},{2,0},{4,2},{6,4},{1,7},{3,1},{5,3},{7,5},{8,14},{10,8},{12,... | collective-permute-start | bytes 983048 | tf_op jit(solution)/shard_map/ppermute | solution.py:119
  40.7 30.7 %collective-permute-start.7 = (bf16[32,5120]{1,0:T(8,128)(2,1)S(1)}, bf16[32,5120]{1,0:T(8,128)(2,1)S(1)}, u32[]{:S(2)}, u32[]{:S(2)}) collective-permute-start(bf16[32,5120]{1,0:T(8,128)(2,1)S(1)} %bitcast.42), channel_id=1, source_target_pairs={{0,2},{2,4},{4,6},{6,0},{1,3},{3,5},{5,7},{7,1},{8,10},{10,12},{12... | collective-permute-start | bytes 983048 | tf_op jit(solution)/shard_map/ppermute | solution.py:116
  40.7 30.7 %collective-permute-start.5 = (bf16[32,5120]{1,0:T(8,128)(2,1)S(1)}, bf16[32,5120]{1,0:T(8,128)(2,1)S(1)}, u32[]{:S(2)}, u32[]{:S(2)}) collective-permute-start(bf16[32,5120]{1,0:T(8,128)(2,1)S(1)} %bitcast.39), channel_id=1, source_target_pairs={{0,2},{2,4},{4,6},{6,0},{1,3},{3,5},{5,7},{7,1},{8,10},{10,12},{12... | collective-permute-start | bytes 983048 | tf_op jit(solution)/shard_map/ppermute | solution.py:118
  40.7 30.8 %collective-permute-start.9 = (bf16[32,5120]{1,0:T(8,128)(2,1)S(1)}, bf16[32,5120]{1,0:T(8,128)(2,1)S(1)}, u32[]{:S(2)}, u32[]{:S(2)}) collective-permute-start(bf16[32,5120]{1,0:T(8,128)(2,1)S(1)} %bitcast.40), channel_id=1, source_target_pairs={{0,6},{2,0},{4,2},{6,4},{1,7},{3,1},{5,3},{7,5},{8,14},{10,8},{12,... | collective-permute-start | bytes 983048 | tf_op jit(solution)/shard_map/ppermute | solution.py:117
  44.3 2.1 %copy-start.1 = (bf16[5120,384]{1,0:T(8,128)(2,1)S(1)}, bf16[5120,384]{1,0:T(8,128)(2,1)}, u32[]{:S(2)}) copy-start(bf16[5120,384]{1,0:T(8,128)(2,1)} %param.14) | copy-start | bytes 11796484
  46.4 2.1 %copy-start.2 = (bf16[5120,384]{1,0:T(8,128)(2,1)S(1)}, bf16[5120,384]{1,0:T(8,128)(2,1)}, u32[]{:S(2)}) copy-start(bf16[5120,384]{1,0:T(8,128)(2,1)} %param.15) | copy-start | bytes 11796484
  71.6 9.2 %collective-permute-start.11 = (bf16[192,5120]{1,0:T(8,128)(2,1)S(1)}, bf16[192,5120]{1,0:T(8,128)(2,1)S(1)}, u32[]{:S(2)}, u32[]{:S(2)}) collective-permute-start(bf16[192,5120]{1,0:T(8,128)(2,1)S(1)} %pad_maximum_fusion), channel_id=1, source_target_pairs={{0,1},{1,0},{2,3},{3,2},{4,5},{5,4},{6,7},{7,6},{8,9},{9,8},{10,11... | collective-permute-start | bytes 5898248 | tf_op jit(solution)/shard_map/ppermute | solution.py:105
  74.4 18.3 %collective-permute-start.8 = (bf16[32,5120]{1,0:T(8,128)(2,1)S(1)}, bf16[32,5120]{1,0:T(8,128)(2,1)S(1)}, u32[]{:S(2)}, u32[]{:S(2)}) collective-permute-start(bf16[32,5120]{1,0:T(8,128)(2,1)S(1)} %collective-permute-done.7), channel_id=1, source_target_pairs={{0,2},{2,4},{4,6},{6,0},{1,3},{3,5},{5,7},{7,1},{8,10},{10,12},{12... | collective-permute-start | bytes 983048 | tf_op jit(solution)/shard_map/ppermute | solution.py:121
  74.5 18.2 %collective-permute-start.10 = (bf16[32,5120]{1,0:T(8,128)(2,1)S(1)}, bf16[32,5120]{1,0:T(8,128)(2,1)S(1)}, u32[]{:S(2)}, u32[]{:S(2)}) collective-permute-start(bf16[32,5120]{1,0:T(8,128)(2,1)S(1)} %collective-permute-done.9), channel_id=1, source_target_pairs={{0,6},{2,0},{4,2},{6,4},{1,7},{3,1},{5,3},{7,5},{8,14},{10,8},{12,... | collective-permute-start | bytes 983048 | tf_op jit(solution)/shard_map/ppermute | solution.py:121
  92.7 2.2 %collective-permute-start.12 = (bf16[64,5120]{1,0:T(8,128)(2,1)S(1)}, bf16[64,5120]{1,0:T(8,128)(2,1)S(1)}, u32[]{:S(2)}, u32[]{:S(2)}) collective-permute-start(bf16[64,5120]{1,0:T(8,128)(2,1)S(1)} %pad_maximum_fusion.3), channel_id=1, source_target_pairs={{0,1},{1,0},{2,3},{3,2},{4,5},{5,4},{6,7},{7,6},{8,9},{9,8},{10,11... | collective-permute-start | bytes 1966088 | tf_op jit(solution)/shard_map/ppermute | solution.py:105

commit v5 on v4

--- a/solution.py
+++ b/solution.py
@@ -18,7 +18,9 @@
 
 
 def ring(by):
-    return [(g, (g + by) % 4) for g in range(4)]
+    return [
+        (g * 2 + c, ((g + (by if c == 0 else -by)) % 4) * 2 + c) for g in range(4) for c in range(2)
+    ]
 
 
 def row_pairs(neighbour):
@@ -113,12 +115,12 @@
     def both_cores(v):
         return jnp.concatenate([v, core_swap(v)], 0)
 
-    prev_a = lax.ppermute(own[:32], "zh", ring(1))
-    nxt_b = lax.ppermute(own[32:], "zh", ring(-1))
-    prev_b = lax.ppermute(own[32:], "zh", ring(1))
-    nxt_a = lax.ppermute(own[:32], "zh", ring(-1))
+    prev_a = lax.ppermute(own[:32], ("zh", "c"), ring(1))
+    nxt_b = lax.ppermute(own[32:], ("zh", "c"), ring(-1))
+    prev_b = lax.ppermute(own[32:], ("zh", "c"), ring(1))
+    nxt_a = lax.ppermute(own[:32], ("zh", "c"), ring(-1))
     own_q = weights_on(own)
-    far = [lax.ppermute(prev_a, "zh", ring(1)), lax.ppermute(nxt_b, "zh", ring(-1))]
+    far = [lax.ppermute(prev_a, ("zh", "c"), ring(1)), lax.ppermute(nxt_b, ("zh", "c"), ring(-1))]
     prev_b, nxt_a, own_q = lax.optimization_barrier((prev_b, nxt_a, own_q))
     prev, nxt = lax.optimization_barrier(
         (jnp.concatenate([prev_a, prev_b], 0), jnp.concatenate([nxt_a, nxt_b], 0))
@@ -130,7 +132,7 @@
     far = jnp.concatenate(far, 0)
     far_q = weights_on(both_cores(far))
     at = [
-        (((zh - d) % 4) * 2 + core) * 64 for core in (c, 1 - c) for d in (0, 1, 3, 2)
+        (((zh - d) % 4) * 2 + core) * 64 for core in (c, 1 - c) for d in (0, 1 + 2 * core, 3 - 2 * core, 2)
     ]
     return attention(jnp.stack(at).astype(jnp.int32), own_q, side_q, near_x, far_q)
 

time: 101 us -> 101 us (level)
  the two profiles are of different devices: /device:TPU:61 before, /device:TPU:57 now
where the time goes in v5:
time: 101 us; the launch traced here: 100 us
  waiting for transfers between devices  39.7 us (39%)
  starting transfers between devices  39.5 us (39%)
  matrix products  11.2 us (11%)
  other arithmetic  3.54 us (4%)
  local copies, waits for them, and re-layouts  3.36 us (3%)
  Pallas kernels  2.74 us (3%)
    ppermute x1, starting transfers between devices, local(): prev_a = lax.ppermute(own[:32], ('zh', 'c'), ring(1))  23 us
    ppermute x1, waiting for transfers between devices, local(): prev_b = lax.ppermute(own[32:], ('zh', 'c'), ring(1))  14.3 us
    dot_general x12, matrix products, weights_on(): jnp.dot(rows, w, preferred_element_type=jnp.float32).astype(jnp.bfloat16)  11.2 us
    ppermute x1, waiting for transfers between devices, local(): lax.ppermute(prev_a, ('zh', 'c'), ring(1))  6.26 us
    ppermute x1, starting transfers between devices, local(): nxt_a = lax.ppermute(own[:32], ('zh', 'c'), ring(-1))  6.03 us
    ppermute x1, waiting for transfers between devices, local(): nxt_b = lax.ppermute(own[32:], ('zh', 'c'), ring(-1))  5.72 us
    ppermute x1, waiting for transfers between devices, local(): out_other = lax.ppermute(outer, ('x', 'zl'), OUTER_PAIRS)  4.6 us
    ppermute x1, waiting for transfers between devices, local(): in_other = lax.ppermute(inner, 'zl', SWAP)  3.98 us
  transfers between devices with their start and end apart: 13, of which 7 were waited for; matrix products, arithmetic and copies ran while one was open for 11% of the time, Pallas kernels for 0%

profile of v5, /device:TPU:57, one launch (start us, length us, event | category | flops | bytes accessed | tf_op | source)
XLA Modules:
  0.0 100.5 jit_solution(13326535316729826587)
XLA Ops:
  0.0 0.8 collective-permute-start
  0.9 1.1 %broadcast_select_fusion.4 = (bf16[2,2,8,5120]{3,2,1,0:T(8,128)(2,1)S(1)}, bf16[2,2,8,5120]{3,2,1,0:T(8,128)(2,1)S(1)}) fusion(pred[]{:T(512)S(6)} %eq.27, bf16[2,2,16,5120]{3,2,1,0:T(8,128)(2,1)} %param.8), kind=kLoop, calls=%fused_computation.31 | loop fusion | flops 327680 | bytes 1310721 | tf_op jit(solution)/shard_map/jit(_where)/select_n | solution.py:79
  2.0 0.7 collective-permute-start.1
  2.7 2.7 %collective-permute-start.3 = (bf16[2,2,8,5120]{3,2,1,0:T(8,128)(2,1)S(1)}, bf16[2,2,8,5120]{3,2,1,0:T(8,128)(2,1)S(1)}, u32[]{:S(2)}, u32[]{:S(2)}) collective-permute-start(bf16[2,2,8,5120]{3,2,1,0:T(8,128)(2,1)S(1)} %get-tuple-element.66), channel_id=1, source_target_pairs={{8,16},{16,8},{40,48},{48,40},{9,17},{17,9},{41,49},{49,41},{10,18... | collective-permute-start | bytes 983048 | tf_op jit(solution)/shard_map/ppermute | solution.py:93
  5.3 0.7 collective-permute-start.2
  6.0 0.1 collective-permute-start.4
  6.2 0.2 dynamic-slice_reduce_fusion.1
  6.4 0.2 fusion.9
  6.6 0.1 fusion.13
  6.8 0.2 fusion.12
  7.1 0.1 stack.35.at
  7.2 0.0 copy-start.3
  7.2 4.6 %collective-permute-done.3 = bf16[2,2,8,5120]{3,2,1,0:T(8,128)(2,1)S(1)} collective-permute-done((bf16[2,2,8,5120]{3,2,1,0:T(8,128)(2,1)S(1)}, bf16[2,2,8,5120]{3,2,1,0:T(8,128)(2,1)S(1)}, u32[]{:S(2)}, u32[]{:S(2)}) %collective-permute-start.3) | collective-permute-done | bytes 327712 | tf_op jit(solution)/shard_map/ppermute | solution.py:93
  11.8 4.0 %collective-permute-done.4 = bf16[2,2,8,5120]{3,2,1,0:T(8,128)(2,1)S(1)} collective-permute-done((bf16[2,2,8,5120]{3,2,1,0:T(8,128)(2,1)S(1)}, bf16[2,2,8,5120]{3,2,1,0:T(8,128)(2,1)S(1)}, u32[]{:S(2)}, u32[]{:S(2)}) %collective-permute-start.4) | collective-permute-done | bytes 327712 | tf_op jit(solution)/shard_map/ppermute | solution.py:94
  15.8 0.1 broadcast_select_fusion.1
  15.9 0.0 copy-start
  15.9 0.9 convert_reduce_fusion
  16.8 0.3 fusion.2
  17.1 0.3 fusion.5
  17.5 6.0 %collective-permute-start.6 = (bf16[32,5120]{1,0:T(8,128)(2,1)S(1)}, bf16[32,5120]{1,0:T(8,128)(2,1)S(1)}, u32[]{:S(2)}, u32[]{:S(2)}) collective-permute-start(bf16[32,5120]{1,0:T(8,128)(2,1)S(1)} %bitcast.41), channel_id=1, source_target_pairs={{0,6},{1,3},{2,0},{3,5},{4,2},{5,7},{6,4},{7,1},{8,14},{9,11},{10,... | collective-permute-start | bytes 983048 | tf_op jit(solution)/shard_map/ppermute | solution.py:121
  23.5 23.0 %collective-permute-start.7 = (bf16[32,5120]{1,0:T(8,128)(2,1)S(1)}, bf16[32,5120]{1,0:T(8,128)(2,1)S(1)}, u32[]{:S(2)}, u32[]{:S(2)}) collective-permute-start(bf16[32,5120]{1,0:T(8,128)(2,1)S(1)} %bitcast.42), channel_id=1, source_target_pairs={{0,2},{1,7},{2,4},{3,1},{4,6},{5,3},{6,0},{7,5},{8,10},{9,15},{10,... | collective-permute-start | bytes 983048 | tf_op jit(solution)/shard_map/ppermute | solution.py:118
  46.6 2.3 %collective-permute-start.5 = (bf16[32,5120]{1,0:T(8,128)(2,1)S(1)}, bf16[32,5120]{1,0:T(8,128)(2,1)S(1)}, u32[]{:S(2)}, u32[]{:S(2)}) collective-permute-start(bf16[32,5120]{1,0:T(8,128)(2,1)S(1)} %bitcast.39), channel_id=1, source_target_pairs={{0,2},{1,7},{2,4},{3,1},{4,6},{5,3},{6,0},{7,5},{8,10},{9,15},{10,... | collective-permute-start | bytes 983048 | tf_op jit(solution)/shard_map/ppermute | solution.py:120
  48.9 0.1 collective-permute-start.9
  48.9 0.7 convolution_convert_fusion.11.refs_0_
  49.6 1.4 %copy-done.1 = bf16[5120,384]{1,0:T(8,128)(2,1)S(1)} copy-done((bf16[5120,384]{1,0:T(8,128)(2,1)S(1)}, bf16[5120,384]{1,0:T(8,128)(2,1)}, u32[]{:S(2)}) %copy-start.1) | copy-done | bytes 3932184
  51.1 0.7 convolution_convert_fusion.10.refs_1_
  51.8 1.4 %copy-done.2 = bf16[5120,384]{1,0:T(8,128)(2,1)S(1)} copy-done((bf16[5120,384]{1,0:T(8,128)(2,1)S(1)}, bf16[5120,384]{1,0:T(8,128)(2,1)}, u32[]{:S(2)}) %copy-start.2) | copy-done | bytes 3932184
  53.2 0.7 convolution_convert_fusion.9.refs_2_
  53.9 14.3 %collective-permute-done.5 = bf16[32,5120]{1,0:T(8,128)(2,1)S(1)} collective-permute-done((bf16[32,5120]{1,0:T(8,128)(2,1)S(1)}, bf16[32,5120]{1,0:T(8,128)(2,1)S(1)}, u32[]{:S(2)}, u32[]{:S(2)}) %collective-permute-start.5) | collective-permute-done | bytes 327712 | tf_op jit(solution)/shard_map/ppermute | solution.py:120
  68.2 5.7 %collective-permute-done.9 = bf16[32,5120]{1,0:T(8,128)(2,1)S(1)} collective-permute-done((bf16[32,5120]{1,0:T(8,128)(2,1)S(1)}, bf16[32,5120]{1,0:T(8,128)(2,1)S(1)}, u32[]{:S(2)}, u32[]{:S(2)}) %collective-permute-start.9) | collective-permute-done | bytes 327712 | tf_op jit(solution)/shard_map/ppermute | solution.py:119
  74.0 0.1 pad_maximum_fusion
  74.1 0.1 collective-permute-start.11
  74.3 0.1 collective-permute-start.8
  74.3 2.4 %collective-permute-start.10 = (bf16[32,5120]{1,0:T(8,128)(2,1)S(1)}, bf16[32,5120]{1,0:T(8,128)(2,1)S(1)}, u32[]{:S(2)}, u32[]{:S(2)}) collective-permute-start(bf16[32,5120]{1,0:T(8,128)(2,1)S(1)} %collective-permute-done.9), channel_id=1, source_target_pairs={{0,6},{1,3},{2,0},{3,5},{4,2},{5,7},{6,4},{7,1},{8,14},{9,11},{10,... | collective-permute-start | bytes 983048 | tf_op jit(solution)/shard_map/ppermute | solution.py:123
  76.7 0.9 convolution_convert_fusion.8.refs_3_
  77.6 0.9 convolution_convert_fusion.7.refs_4_
  78.6 0.9 convolution_convert_fusion.6.refs_5_
  79.5 1.3 %convolution_convert_fusion.2.refs_6_ = bf16[192,384]{1,0:T(8,128)(2,1)S(1)} fusion(bf16[192,5120]{1,0:T(8,128)(2,1)S(1)} %collective-permute-done.11, bf16[5120,384]{1,0:T(8,128)(2,1)S(1)} %copy-done), kind=kOutput, calls=%fused_computation.14 | convolution fusion | flops 755048448 | bytes 6045696 | tf_op jit(solution)/shard_map/dot_general | solution.py:111
  80.7 1.3 %convolution_convert_fusion.1.refs_7_ = bf16[192,384]{1,0:T(8,128)(2,1)S(1)} fusion(bf16[192,5120]{1,0:T(8,128)(2,1)S(1)} %collective-permute-done.11, bf16[5120,384]{1,0:T(8,128)(2,1)S(1)} %copy-done.1), kind=kOutput, calls=%fused_computation.13 | convolution fusion | flops 755048448 | bytes 6045696 | tf_op jit(solution)/shard_map/dot_general | solution.py:111
  82.0 1.2 %convolution_convert_fusion.refs_8_ = bf16[192,384]{1,0:T(8,128)(2,1)S(1)} fusion(bf16[192,5120]{1,0:T(8,128)(2,1)S(1)} %collective-permute-done.11, bf16[5120,384]{1,0:T(8,128)(2,1)S(1)} %copy-done.2), kind=kOutput, calls=%fused_computation.12 | convolution fusion | flops 755048448 | bytes 6045696 | tf_op jit(solution)/shard_map/dot_general | solution.py:111
  83.2 6.3 %collective-permute-done.8 = bf16[32,5120]{1,0:T(8,128)(2,1)S(1)} collective-permute-done((bf16[32,5120]{1,0:T(8,128)(2,1)S(1)}, bf16[32,5120]{1,0:T(8,128)(2,1)S(1)}, u32[]{:S(2)}, u32[]{:S(2)}) %collective-permute-start.8) | collective-permute-done | bytes 327712 | tf_op jit(solution)/shard_map/ppermute | solution.py:123
  89.5 3.1 %collective-permute-done.10 = bf16[32,5120]{1,0:T(8,128)(2,1)S(1)} collective-permute-done((bf16[32,5120]{1,0:T(8,128)(2,1)S(1)}, bf16[32,5120]{1,0:T(8,128)(2,1)S(1)}, u32[]{:S(2)}, u32[]{:S(2)}) %collective-permute-start.10) | collective-permute-done | bytes 327712 | tf_op jit(solution)/shard_map/ppermute | solution.py:123
  92.7 0.6 collective-permute-start.12
  93.3 1.7 %collective-permute-done.12 = bf16[64,5120]{1,0:T(8,128)(2,1)S(1)} collective-permute-done((bf16[64,5120]{1,0:T(8,128)(2,1)S(1)}, bf16[64,5120]{1,0:T(8,128)(2,1)S(1)}, u32[]{:S(2)}, u32[]{:S(2)}) %collective-permute-start.12) | collective-permute-done | bytes 655392 | tf_op jit(solution)/shard_map/ppermute | solution.py:107
  95.0 0.9 convolution_convert_fusion.5.refs_9_
  95.9 0.9 convolution_convert_fusion.4.refs_10_
  96.8 0.9 convolution_convert_fusion.3.refs_11_
  97.8 2.7 %shard_map.82 = bf16[512,384]{1,0:T(8,128)(2,1)} custom-call(s32[8]{0:T(128)S(1)} %stack.35.at, bf16[64,384]{1,0:T(8,128)(2,1)S(1)} %convolution_convert_fusion.11.refs_0_, bf16[64,384]{1,0:T(8,128)(2,1)S(1)} %convolution_convert_fusion.10.refs_1_, bf16[64,384]{1,0:T(8,128)(2,1)S(1)} %convolution_convert_fusion.9.refs_2_, ...), custom_call_target="tpu_custom_call" | custom-call | tf_op jit(solution)/shard_map/pallas_call | solution.py:171
  (33 shorter events, 0.4 us)
Async XLA Ops:
  0.0 6.2 %copy-start.6 = (s32[32,16]{0,1:T(8,128)S(1)}, s32[32,16]{0,1:T(8,128)}, u32[]{:S(2)}) copy-start(s32[32,16]{0,1:T(8,128)} %param.9) | copy-start | bytes 6148
  0.0 6.8 %copy-start.7 = (s32[32,16]{0,1:T(8,128)S(1)}, s32[32,16]{0,1:T(8,128)}, u32[]{:S(2)}) copy-start(s32[32,16]{0,1:T(8,128)} %param.10) | copy-start | bytes 6148
  0.0 7.1 %copy-start.4 = (f32[5120]{0:T(1024)S(1)}, f32[5120]{0:T(1024)}, u32[]{:S(2)}) copy-start(f32[5120]{0:T(1024)} %param.12) | copy-start | bytes 61444
  0.0 15.8 %collective-permute-start = (bf16[2,2,16,5120]{3,2,1,0:T(8,128)(2,1)}, bf16[2,2,16,5120]{3,2,1,0:T(8,128)(2,1)S(1)}, u32[]{:S(2)}, u32[]{:S(2)}) collective-permute-start(bf16[2,2,16,5120]{3,2,1,0:T(8,128)(2,1)} %param.8), channel_id=1, source_target_pairs={{7,32},{32,7},{15,40},{40,15},{23,48},{48,23},{31,56},{56,31},{39,... | collective-permute-start | bytes 1966088 | tf_op jit(solution)/shard_map/ppermute | solution.py:90
  2.0 5.2 %collective-permute-start.1 = (bf16[2,2,8,5120]{3,2,1,0:T(8,128)(2,1)S(1)}, bf16[2,2,8,5120]{3,2,1,0:T(8,128)(2,1)S(1)}, u32[]{:S(2)}, u32[]{:S(2)}) collective-permute-start(bf16[2,2,8,5120]{3,2,1,0:T(8,128)(2,1)S(1)} %get-tuple-element.66), channel_id=1, source_target_pairs={{23,40},{48,15},{15,48},{40,23},{55,72},{80,47},{47,80},{72,55},{8... | collective-permute-start | bytes 983048 | tf_op jit(solution)/shard_map/ppermute | solution.py:91
  2.7 9.1 %collective-permute-start.3 = (bf16[2,2,8,5120]{3,2,1,0:T(8,128)(2,1)S(1)}, bf16[2,2,8,5120]{3,2,1,0:T(8,128)(2,1)S(1)}, u32[]{:S(2)}, u32[]{:S(2)}) collective-permute-start(bf16[2,2,8,5120]{3,2,1,0:T(8,128)(2,1)S(1)} %get-tuple-element.66), channel_id=1, source_target_pairs={{8,16},{16,8},{40,48},{48,40},{9,17},{17,9},{41,49},{49,41},{10,18... | collective-permute-start | bytes 983048 | tf_op jit(solution)/shard_map/ppermute | solution.py:93
  5.3 1.8 %collective-permute-start.2 = (bf16[2,2,8,5120]{3,2,1,0:T(8,128)(2,1)S(1)}, bf16[2,2,8,5120]{3,2,1,0:T(8,128)(2,1)S(1)}, u32[]{:S(2)}, u32[]{:S(2)}) collective-permute-start(bf16[2,2,8,5120]{3,2,1,0:T(8,128)(2,1)S(1)} %get-tuple-element.65), channel_id=1, source_target_pairs={{15,32},{40,7},{7,40},{32,15},{31,48},{56,23},{23,56},{48,31},{47,... | collective-permute-start | bytes 983048 | tf_op jit(solution)/shard_map/ppermute | solution.py:92
  6.0 9.7 %collective-permute-start.4 = (bf16[2,2,8,5120]{3,2,1,0:T(8,128)(2,1)S(1)}, bf16[2,2,8,5120]{3,2,1,0:T(8,128)(2,1)S(1)}, u32[]{:S(2)}, u32[]{:S(2)}) collective-permute-start(bf16[2,2,8,5120]{3,2,1,0:T(8,128)(2,1)S(1)} %get-tuple-element.65), channel_id=1, source_target_pairs={{0,8},{8,0},{1,9},{9,1},{2,10},{10,2},{3,11},{11,3},{4,12},{12,4},... | collective-permute-start | bytes 983048 | tf_op jit(solution)/shard_map/ppermute | solution.py:94
  7.2 8.7 %copy-start.3 = (bf16[2,2,16,5120]{3,2,1,0:T(8,128)(2,1)S(1)}, bf16[2,2,16,5120]{3,2,1,0:T(8,128)(2,1)}, u32[]{:S(2)}) copy-start(bf16[2,2,16,5120]{3,2,1,0:T(8,128)(2,1)} %param.8) | copy-start | bytes 1966084
  15.9 1.3 %copy-start.5 = (f32[5120]{0:T(1024)S(1)}, f32[5120]{0:T(1024)}, u32[]{:S(2)}) copy-start(f32[5120]{0:T(1024)} %param.11) | copy-start | bytes 61444
  15.9 33.1 %copy-start = (bf16[5120,384]{1,0:T(8,128)(2,1)S(1)}, bf16[5120,384]{1,0:T(8,128)(2,1)}, u32[]{:S(2)}) copy-start(bf16[5120,384]{1,0:T(8,128)(2,1)} %param.13) | copy-start | bytes 11796484
  17.5 50.6 %collective-permute-start.6 = (bf16[32,5120]{1,0:T(8,128)(2,1)S(1)}, bf16[32,5120]{1,0:T(8,128)(2,1)S(1)}, u32[]{:S(2)}, u32[]{:S(2)}) collective-permute-start(bf16[32,5120]{1,0:T(8,128)(2,1)S(1)} %bitcast.41), channel_id=1, source_target_pairs={{0,6},{1,3},{2,0},{3,5},{4,2},{5,7},{6,4},{7,1},{8,14},{9,11},{10,... | collective-permute-start | bytes 983048 | tf_op jit(solution)/shard_map/ppermute | solution.py:121
  23.5 44.6 %collective-permute-start.7 = (bf16[32,5120]{1,0:T(8,128)(2,1)S(1)}, bf16[32,5120]{1,0:T(8,128)(2,1)S(1)}, u32[]{:S(2)}, u32[]{:S(2)}) collective-permute-start(bf16[32,5120]{1,0:T(8,128)(2,1)S(1)} %bitcast.42), channel_id=1, source_target_pairs={{0,2},{1,7},{2,4},{3,1},{4,6},{5,3},{6,0},{7,5},{8,10},{9,15},{10,... | collective-permute-start | bytes 983048 | tf_op jit(solution)/shard_map/ppermute | solution.py:118
  46.6 21.6 %collective-permute-start.5 = (bf16[32,5120]{1,0:T(8,128)(2,1)S(1)}, bf16[32,5120]{1,0:T(8,128)(2,1)S(1)}, u32[]{:S(2)}, u32[]{:S(2)}) collective-permute-start(bf16[32,5120]{1,0:T(8,128)(2,1)S(1)} %bitcast.39), channel_id=1, source_target_pairs={{0,2},{1,7},{2,4},{3,1},{4,6},{5,3},{6,0},{7,5},{8,10},{9,15},{10,... | collective-permute-start | bytes 983048 | tf_op jit(solution)/shard_map/ppermute | solution.py:120
  48.9 25.1 %collective-permute-start.9 = (bf16[32,5120]{1,0:T(8,128)(2,1)S(1)}, bf16[32,5120]{1,0:T(8,128)(2,1)S(1)}, u32[]{:S(2)}, u32[]{:S(2)}) collective-permute-start(bf16[32,5120]{1,0:T(8,128)(2,1)S(1)} %bitcast.40), channel_id=1, source_target_pairs={{0,6},{1,3},{2,0},{3,5},{4,2},{5,7},{6,4},{7,1},{8,14},{9,11},{10,... | collective-permute-start | bytes 983048 | tf_op jit(solution)/shard_map/ppermute | solution.py:119
  48.9 2.1 %copy-start.1 = (bf16[5120,384]{1,0:T(8,128)(2,1)S(1)}, bf16[5120,384]{1,0:T(8,128)(2,1)}, u32[]{:S(2)}) copy-start(bf16[5120,384]{1,0:T(8,128)(2,1)} %param.14) | copy-start | bytes 11796484
  51.1 2.1 %copy-start.2 = (bf16[5120,384]{1,0:T(8,128)(2,1)S(1)}, bf16[5120,384]{1,0:T(8,128)(2,1)}, u32[]{:S(2)}) copy-start(bf16[5120,384]{1,0:T(8,128)(2,1)} %param.15) | copy-start | bytes 11796484
  74.1 5.4 %collective-permute-start.11 = (bf16[192,5120]{1,0:T(8,128)(2,1)S(1)}, bf16[192,5120]{1,0:T(8,128)(2,1)S(1)}, u32[]{:S(2)}, u32[]{:S(2)}) collective-permute-start(bf16[192,5120]{1,0:T(8,128)(2,1)S(1)} %pad_maximum_fusion), channel_id=1, source_target_pairs={{0,1},{1,0},{2,3},{3,2},{4,5},{5,4},{6,7},{7,6},{8,9},{9,8},{10,11... | collective-permute-start | bytes 5898248 | tf_op jit(solution)/shard_map/ppermute | solution.py:107
  74.3 15.3 %collective-permute-start.8 = (bf16[32,5120]{1,0:T(8,128)(2,1)S(1)}, bf16[32,5120]{1,0:T(8,128)(2,1)S(1)}, u32[]{:S(2)}, u32[]{:S(2)}) collective-permute-start(bf16[32,5120]{1,0:T(8,128)(2,1)S(1)} %collective-permute-done.7), channel_id=1, source_target_pairs={{0,2},{1,7},{2,4},{3,1},{4,6},{5,3},{6,0},{7,5},{8,10},{9,15},{10,... | collective-permute-start | bytes 983048 | tf_op jit(solution)/shard_map/ppermute | solution.py:123
  74.3 18.3 %collective-permute-start.10 = (bf16[32,5120]{1,0:T(8,128)(2,1)S(1)}, bf16[32,5120]{1,0:T(8,128)(2,1)S(1)}, u32[]{:S(2)}, u32[]{:S(2)}) collective-permute-start(bf16[32,5120]{1,0:T(8,128)(2,1)S(1)} %collective-permute-done.9), channel_id=1, source_target_pairs={{0,6},{1,3},{2,0},{3,5},{4,2},{5,7},{6,4},{7,1},{8,14},{9,11},{10,... | collective-permute-start | bytes 983048 | tf_op jit(solution)/shard_map/ppermute | solution.py:123
  92.7 2.3 %collective-permute-start.12 = (bf16[64,5120]{1,0:T(8,128)(2,1)S(1)}, bf16[64,5120]{1,0:T(8,128)(2,1)S(1)}, u32[]{:S(2)}, u32[]{:S(2)}) collective-permute-start(bf16[64,5120]{1,0:T(8,128)(2,1)S(1)} %pad_maximum_fusion.3), channel_id=1, source_target_pairs={{0,1},{1,0},{2,3},{3,2},{4,5},{5,4},{6,7},{7,6},{8,9},{9,8},{10,11... | collective-permute-start | bytes 1966088 | tf_op jit(solution)/shard_map/ppermute | solution.py:107
